TPU v7x, 32 devices: a whole 2x2x4 slice. The times are simulated.
32 devices in a mesh: group: 4 (over y, x), cluster: 8 (over z, core).
Axes of the slice: x: 2, y: 2, z: 4, core: 2. Of those that a mesh axis runs over, the one named last changes fastest.
Arguments:
- charges: float32 [262144, 128], P(('group', 'cluster')), may hold values from -6 to 6
- leaf_size: int32 [1024], P(('group', 'cluster')), may hold values from 1 to 256, 196608 in all
- leaf_basis: float32 [1024, 64, 256], P(('group', 'cluster')), may hold values from -0.375 to 0.375
- leaf_transfer: float32 [1024, 64, 64], P(('group', 'cluster')), may hold values from -0.375 to 0.375
- mid_transfer: float32 [256, 64, 64], P(('group', 'cluster')), may hold values from -0.25 to 0.25
- leaf_parent: int32 [1024], P(('group', 'cluster')), may hold values from 0 to 7, as said below
- send_leaf: int32 [2048], P(('group', 'cluster')), may hold values from 0 to 32, as said below
- pair_leaf: int32 [1024, 12], P(('group', 'cluster')), may hold values from 0 to 64, as said below
- leaf_coupling: float32 [1024, 64, 768], P(('group', 'cluster')), may hold values from -0.21875 to 0.21875
- send_mid: int32 [2048], P(('group', 'cluster')), may hold values from 0 to 8, as said below
- pair_mid: int32 [256, 32], P(('group', 'cluster')), may hold values from 0 to 64, as said below
- mid_coupling: float32 [256, 64, 2048], P(('group', 'cluster')), may hold values from -0.125 to 0.125
- top_pairs: int32 [32, 4], P('group'), may hold values from 0 to 32, as said below
- top_coupling: float32 [32, 64, 256], P('group'), may hold values from -0.375 to 0.375
Outputs:
- far_field: float32 [262144, 128], P(('group', 'cluster'))
Inputs may be any that keep to these rules, and one draw needn't show every extreme that they name: `send_leaf`: entry (d * 32 + r) * 2 + j is the leaf, local to device d, whose block d puts in slot j for device r, or 32 for an empty slot; the leaves in one sender's slots to one receiver are distinct; some receiver has every slot from every sender filled. `pair_leaf`: row t names leaf t's admissible partners as positions 2 * d + j among the slots its owner receives, filled slots only and distinct within a row, or 64 for no partner; every filled slot is named by some row of its receiver. `send_mid`: as send_leaf, for level-one clusters: local indices below 8, 8 for an empty slot; some receiver has every slot from every sender filled. `pair_mid`: as pair_leaf, for level-one clusters; every filled slot is named by some row of its receiver. `leaf_parent`: every level-one cluster of a device is the parent of at least one of its leaves. `top_pairs`: row o names coarse clusters other than o, distinct within a row, at least one a row, or 32 for no partner.
All inputs are finite; a program needn't handle non-finite values. No bound on the sum of `leaf_size` on one device may be relied on, other than what follows from the above.
Results may differ from a plain program's by a relative error of at most 0.000062.
Values sent between devices are 32-bit elements; how exact they have to be, the bound alone decides.
No kernel may reach another device: no remote copies, remote signals or barrier semaphores. Data moves between devices by JAX's collectives and lax.ppermute only.
A program may use at most 128 MiB of HBM per device.

v0:
```python
import functools
import math

import jax
import jax.numpy as jnp
from jax import lax
from jax.experimental import pallas as pl
from jax.experimental.pallas import tpu as pltpu
from jax.sharding import PartitionSpec as P

AXES = ("group", "cluster")
MIB = 1024 * 1024


def params(size):
    return pltpu.CompilerParams(vmem_limit_bytes=size)


def cost(flops, size):
    return pl.CostEstimate(flops=flops, bytes_accessed=size, transcendentals=0)


def whole(shape):
    return pl.BlockSpec(shape, lambda i, *_: (0,) * len(shape), pipeline_mode=pl.Buffered(1))


def first(group, *rest):
    return pl.BlockSpec((group,) + rest, lambda i, *_: (i,) + (0,) * len(rest))


def split(x):
    high = x.astype(jnp.bfloat16)
    low = (x - high.astype(jnp.float32)).astype(jnp.bfloat16)
    return high, low


def rows_of(x):
    return jnp.concatenate(split(x), axis=0)


def lanes_of(x):
    return jnp.concatenate(split(x), axis=1)


def dot(a, b):
    return lax.dot_general(a, b, (((1,), (0,)), ((), ())), preferred_element_type=jnp.float32)


def fold(product):
    m, n = product.shape[0] // 2, product.shape[1] // 2
    return product[:m, :n] + (product[:m, n:] + product[m:, :n] + product[m:, n:])


def deep_dot(a, b):
    high, low = split(b)
    return dot(jnp.concatenate([a, a], axis=1), jnp.concatenate([high, high, low, low], axis=0))


def up_kernel(
    sizes, size, parent, slots, group_at, lane_at, charges, basis, transfer, mid_transfer, send, coef, up,
    *messages
):
    step = pl.program_id(0)
    group, rank, points = basis.shape
    mids = mid_transfer.shape[0]
    ports = up.shape[1]

    @pl.when(step == 0)
    def _():
        up[: mids * rank, :] = jnp.zeros((mids * rank, ports), jnp.float32)
        up[(mids + 1) * rank :, :] = jnp.zeros((up.shape[0] - (mids + 1) * rank, ports), jnp.float32)
        for row in range(send.shape[0]):
            spot = (mids + 1) * rank + row
            up[spot : spot + 1, : send.shape[1]] = send[row : row + 1, :].astype(jnp.float32)

    point = lax.broadcasted_iota(jnp.int32, (points, ports), 0)
    values = []
    for g in range(group):
        block = jnp.where(
            point < size[step * group + g], charges[g * points : (g + 1) * points, :], 0.0
        )
        values.append(fold(dot(rows_of(basis[g]), lanes_of(block))))
    for g in range(group):
        coef[g] = values[g]
    moved = [fold(dot(rows_of(transfer[g]), lanes_of(values[g]))) for g in range(group)]
    for g in range(group):
        where = pl.ds(pl.multiple_of(parent[step * group + g] * rank, rank), rank)
        up[where, :] += moved[g]

    @pl.when(step == pl.num_programs(0) - 1)
    def _():
        terms = [
            fold(dot(rows_of(mid_transfer[c]), lanes_of(up[c * rank : (c + 1) * rank, :])))
            for c in range(mids)
        ]
        while len(terms) > 1:
            terms = [sum(terms[i : i + 2]) for i in range(0, len(terms), 2)]
        up[mids * rank : (mids + 1) * rank, :] = terms[0]
        per_cluster, per_pair = sizes
        for d, message in enumerate(messages):
            for side in range(2):
                receiver = (group_at[0] ^ d) * per_cluster + (lane_at[0] ^ side)
                for j in range(per_pair):
                    block = jnp.clip(slots[receiver * per_pair + j], 0, mids - 1)
                    source = pl.ds(pl.multiple_of(block * rank, rank), rank)
                    message[(1 - side) * (per_pair + 1) + j] = up[source, :]
            message[per_pair] = terms[0]


def up_sweep(
    sizes, groups, group_at, lane_at, charges, leaf_size, basis, transfer, mid_transfer, leaf_parent, slots
):
    leaves, rank, points = basis.shape
    ports = charges.shape[1]
    mids = mid_transfer.shape[0]
    group = 8
    send_mid = slots.reshape(-1, min(slots.shape[0], ports))
    up_rows = (mids + 1) * rank + -(-send_mid.shape[0] // 8) * 8
    message = (2 * sizes[1] + 1, rank, ports)
    return pl.pallas_call(
        functools.partial(up_kernel, sizes),
        grid_spec=pltpu.PrefetchScalarGridSpec(
            num_scalar_prefetch=5,
            grid=(leaves // group,),
            in_specs=[
                first(group * points, ports),
                first(group, rank, points),
                first(group, rank, rank),
                whole(mid_transfer.shape),
                whole(send_mid.shape),
            ],
            out_specs=[first(group, rank, ports), whole((up_rows, ports))] + [whole(message)] * groups,
        ),
        out_shape=[
            jax.ShapeDtypeStruct((leaves, rank, ports), jnp.float32),
            jax.ShapeDtypeStruct((up_rows, ports), jnp.float32),
        ]
        + [jax.ShapeDtypeStruct(message, jnp.float32)] * groups,
        compiler_params=params(60 * MIB),
        cost_estimate=cost(10**9, 10**7),
        name="up_sweep",
    )(
        leaf_size, leaf_parent, slots, group_at, lane_at, charges, basis, transfer, mid_transfer, send_mid
    )


def spread_kernel(send, coef, out):
    leaves = coef.shape[0]

    @pl.loop(0, out.shape[0], unroll=8)
    def _(slot):
        out[slot] = coef[jnp.minimum(send[slot], leaves - 1)]


def spread(send_leaf, coef):
    vmem = pl.BlockSpec(memory_space=pltpu.VMEM)
    shape = (send_leaf.shape[0],) + coef.shape[1:]
    return pl.pallas_call(
        spread_kernel,
        in_specs=[pl.BlockSpec(memory_space=pltpu.SMEM), vmem],
        out_specs=vmem,
        out_shape=jax.ShapeDtypeStruct(shape, jnp.float32),
        compiler_params=params(60 * MIB),
        cost_estimate=cost(0, 4 * 10**6),
        name="spread",
    )(send_leaf, coef)


def select_kernel(sizes, group_at, lane_at, *refs):
    lines, per_cluster, up_rows, mids, rank, per_pair, groups = sizes
    received, messages = refs[:lines], refs[lines : lines + groups]
    payloads, tables, sem, table_sem = refs[lines + groups :]
    group, lane = group_at[0], lane_at[0]
    table_rows = up_rows - (mids + 1) * rank
    ports = payloads.shape[2]
    copies = []
    for line, ref in enumerate(received):
        table = ref.at[pl.ds((mids + 1) * rank, table_rows), :]
        copies.append(pltpu.make_async_copy(table, tables.at[line], table_sem.at[line]))
        copies.append(pltpu.make_async_copy(ref, payloads.at[line], sem.at[line]))
    for copy in copies:
        copy.start()
    for copy in copies:
        copy.wait()
    for d, message in enumerate(messages):
        for side in range(2):
            receiver = (group ^ d) * per_cluster + (lane ^ side)

            @pl.loop(0, lines, unroll=min(lines, 4))
            def _(line):
                for j in range(per_pair):
                    entry = receiver * per_pair + j
                    listed = tables[line, lax.div(entry, ports), lax.rem(entry, ports)]
                    block = jnp.clip(listed.astype(jnp.int32), 0, mids - 1)
                    target = (1 - side) * (per_pair + 1) * lines + line * per_pair + j
                    message[target] = payloads[line, pl.ds(pl.multiple_of(block * rank, 8), rank), :]

        for line in range(lines):
            message[lines * per_pair + line] = payloads[line, mids * rank : (mids + 1) * rank, :]


def select(sizes, group_at, lane_at, received):
    lines, per_cluster, up_rows, mids, rank, per_pair, groups = sizes
    ports = received[0].shape[1]
    table_rows = up_rows - (mids + 1) * rank
    payloads = (lines, up_rows, ports)
    shape = jax.ShapeDtypeStruct((lines * (2 * per_pair + 1), rank, ports), jnp.float32)
    return pl.pallas_call(
        functools.partial(select_kernel, sizes),
        in_specs=[pl.BlockSpec(memory_space=pltpu.SMEM)] * 2
        + [pl.BlockSpec(memory_space=pl.ANY)] * len(received),
        out_specs=[pl.BlockSpec(memory_space=pltpu.VMEM)] * groups,
        out_shape=[shape] * groups,
        scratch_shapes=[
            pltpu.VMEM(payloads, jnp.float32),
            pltpu.SMEM((lines, table_rows, ports), jnp.float32),
            pltpu.SemaphoreType.DMA((lines,)),
            pltpu.SemaphoreType.DMA((lines,)),
        ],
        compiler_params=params(60 * MIB),
        cost_estimate=cost(0, 4 * 10**6),
        name="select",
    )(group_at, lane_at, *received)


def prepare_kernel(after, coupling, basis, transfer, mid_coupling, mid_transfer, wide, basis_t, mid_wide):
    for g in range(coupling.shape[0]):
        wide[g] = rows_of(jnp.concatenate([coupling[g], transfer[g].T], axis=1))
        basis_t[g] = rows_of(basis[g]).T
    for g in range(mid_coupling.shape[0]):
        mid_wide[g] = rows_of(jnp.concatenate([mid_coupling[g], mid_transfer[g].T], axis=1))


def prepare(after, coupling, basis, transfer, mid_coupling, mid_transfer):
    leaves, rank, width = coupling.shape
    points = basis.shape[2]
    mids, _, mid_width = mid_coupling.shape
    steps = mids
    group = leaves // steps
    shapes = [
        (leaves, 2 * rank, width + rank),
        (leaves, points, 2 * rank),
        (mids, 2 * rank, mid_width + rank),
    ]
    return pl.pallas_call(
        prepare_kernel,
        grid=(steps,),
        in_specs=[
            pl.BlockSpec(memory_space=pl.ANY),
            first(group, rank, width),
            first(group, rank, points),
            first(group, rank, rank),
            first(1, rank, mid_width),
            first(1, rank, rank),
        ],
        out_specs=[first(s[0] // steps, *s[1:]) for s in shapes],
        out_shape=[jax.ShapeDtypeStruct(s, jnp.bfloat16) for s in shapes],
        compiler_params=params(60 * MIB),
        cost_estimate=cost(0, 3 * 10**7),
        name="prepare",
    )(after, coupling, basis, transfer, mid_coupling, mid_transfer)


def tail_kernel(sizes, parent, pair, position, tops, size, pair_leaf, *refs):
    bounds, per_pair, groups, chunk, group, ahead = sizes
    lines, count = bounds[-1], (len(bounds) - 1) * groups
    messages = refs[: 2 * count]
    arrived, mid_wide, top_coupling, wide, basis, out = refs[2 * count : 2 * count + 6]
    scratch = refs[2 * count + 6 :]
    held_messages, scratch = scratch[: 2 * count], scratch[2 * count :]
    (
        arrived_held, mid_wide_held, top_held, wide_held, basis_held, parts, top_parts, leaf_parts, out_held,
        message_sem, arrived_sem, mid_sem, top_sem, wide_sem, basis_sem, out_sem,
    ) = scratch
    mids, leaves, points = mid_wide.shape[0], wide.shape[0], basis.shape[1]
    slots, top_count = arrived.shape[0], top_parts.shape[0] - 1
    ports = out.shape[1]
    steps, chunks = leaves // group, slots // chunk

    def fetch_message(index):
        held = held_messages[index]
        start = 0 if index >= count else messages[index].shape[0] - held.shape[0]
        source = messages[index].at[pl.ds(start, held.shape[0])]
        return pltpu.make_async_copy(source, held, message_sem.at[index])

    def fetch_arrived(index):
        source = arrived.at[pl.ds(index * chunk, chunk)]
        return pltpu.make_async_copy(source, arrived_held.at[index % 2], arrived_sem.at[index % 2])

    def fetch_mid(c):
        return pltpu.make_async_copy(mid_wide.at[c], mid_wide_held.at[c], mid_sem.at[c])

    def fetch_leaves(index):
        some = pl.ds(index * group, group)
        return (
            pltpu.make_async_copy(wide.at[some], wide_held.at[some], wide_sem.at[index]),
            pltpu.make_async_copy(basis.at[some], basis_held.at[some], basis_sem.at[index]),
        )

    fetch_top = pltpu.make_async_copy(top_coupling.at[position[0]], top_held, top_sem)
    for index in range(min(2, chunks)):
        fetch_arrived(index).start()
    for c in range(mids // 2):
        fetch_mid(c).start()
    for index in range(2 * count):
        fetch_message(index).start()
    fetch_top.start()
    for c in range(mids // 2, mids):
        fetch_mid(c).start()

    leaf_parts[slots] = jnp.zeros(leaf_parts.shape[1:], jnp.bfloat16)
    parts[slots] = jnp.zeros(parts.shape[1:], jnp.bfloat16)
    top_parts[top_count] = jnp.zeros(top_parts.shape[1:], jnp.bfloat16)
    for index in range(chunks):
        fetch_arrived(index).wait()
        @pl.loop(0, chunk, unroll=8)
        def _(slot):
            leaf_parts[index * chunk + slot] = lanes_of(arrived_held[index % 2, slot])

        if index + 2 < chunks:
            fetch_arrived(index + 2).start()

    for index in range(2 * count):
        side, message = divmod(index, count)
        batch, d = divmod(message, groups)
        lines_held = bounds[batch + 1] - bounds[batch]
        piece = lines_held * per_pair
        base = (d * 2 + side) * lines + bounds[batch]
        held = held_messages[index]
        first_slot, first_top = (lines_held, 0) if side == 0 else (0, piece)
        fetch_message(index).wait()

        @pl.loop(0, piece, unroll=min(piece, 6))
        def _(slot):
            parts[base * per_pair + slot] = lanes_of(held[first_slot + slot])

        for line in range(lines_held):
            top_parts[base + line] = lanes_of(held[first_top + line])

    for index in range(ahead):
        for copy in fetch_leaves(index):
            copy.start()
    fetch_top.wait()
    stacked = jnp.concatenate([top_parts[tops[k]] for k in range(tops.shape[0])], axis=0)
    parts[slots + 1] = lanes_of(fold(dot(rows_of(top_held[...]), stacked)))
    for c in range(mids):
        fetch_mid(c).wait()

    @pl.loop(0, mids, step=4)
    def _(start):
        values = []
        for g in range(4):
            blocks = [parts[pair[start + g, k]] for k in range(pair.shape[1])] + [parts[slots + 1]]
            values.append(fold(dot(mid_wide_held[start + g], jnp.concatenate(blocks, axis=0))))
        for g in range(4):
            leaf_parts[slots + 1 + start + g] = lanes_of(values[g])

    point = lax.broadcasted_iota(jnp.int32, (points, ports), 0)

    def send(index):
        rows = group * points
        target = out.at[pl.ds(index * rows, rows), :]
        return pltpu.make_async_copy(out_held.at[index % 2], target, out_sem.at[index % 2])

    for index in range(steps):
        if index + ahead < steps:
            for copy in fetch_leaves(index + ahead):
                copy.start()
        for copy in fetch_leaves(index):
            copy.wait()
        values = []
        for g in range(group):
            leaf = index * group + g
            blocks = [leaf_parts[pair_leaf[leaf, k]] for k in range(pair_leaf.shape[1])]
            blocks.append(leaf_parts[slots + 1 + parent[leaf]])
            values.append(fold(dot(wide_held[leaf], jnp.concatenate(blocks, axis=0))))
        if index >= 2:
            send(index - 2).wait()
        for g in range(group):
            far = deep_dot(basis_held[index * group + g], values[g])
            far = jnp.where(point < size[index * group + g], far, 0.0)
            out_held[index % 2, g * points : (g + 1) * points, :] = far
        send(index).start()
    for index in range(max(0, steps - 2), steps):
        send(index).wait()


def tail(
    bounds, per_pair, groups, parent, pair, position, tops, size, pair_leaf, near_side, far_side, arrived,
    mid_wide, top_coupling, wide, basis
):
    mids = mid_wide.shape[0]
    leaves, points, _ = basis.shape
    slots, rank, ports = arrived.shape
    owners = slots // per_pair
    group, chunk, ahead = 4, min(slots, 32), 3
    held = []
    for message in range(len(near_side)):
        batch = message // groups
        held.append((bounds[batch + 1] - bounds[batch]) * (per_pair + 1))
    full, half = jnp.float32, jnp.bfloat16
    scratch = [((h, rank, ports), full) for h in held + held] + [
        ((2, chunk, rank, ports), full),
        (mid_wide.shape, half),
        (top_coupling.shape[1:], full),
        (wide.shape, half),
        (basis.shape, half),
        ((slots + 2, rank, 2 * ports), half),
        ((owners + 1, rank, 2 * ports), half),
        ((slots + 1 + mids, rank, 2 * ports), half),
        ((2, group * points, ports), full),
    ]
    semaphores = [(2 * len(near_side),), (2,), (mids,), (), (leaves // group,), (leaves // group,), (2,)]
    scalars = (parent, pair, position, tops, size, pair_leaf)
    pin = functools.partial(pltpu.with_memory_space_constraint, memory_space=pltpu.HBM)
    matrices = (mid_wide, top_coupling, wide, basis)
    arrays = (*map(pin, near_side), *map(pin, far_side), arrived, *map(pin, matrices))
    used = sum(jnp.dtype(dtype).itemsize * math.prod(shape) for shape, dtype in scratch)
    return pl.pallas_call(
        functools.partial(tail_kernel, (bounds, per_pair, groups, chunk, group, ahead)),
        in_specs=[pl.BlockSpec(memory_space=pltpu.SMEM)] * len(scalars)
        + [pl.BlockSpec(memory_space=pl.ANY)] * len(arrays),
        out_specs=pl.BlockSpec(memory_space=pl.ANY),
        out_shape=jax.ShapeDtypeStruct((leaves * points, ports), full),
        scratch_shapes=[pltpu.VMEM(shape, dtype) for shape, dtype in scratch]
        + [pltpu.SemaphoreType.DMA(n) for n in semaphores],
        compiler_params=params(min(60 * MIB, used + 6 * MIB)),
        cost_estimate=cost(6 * 10**9, 2 * 10**7),
        name="tail",
    )(*scalars, *arrays)


def body(
    charges, leaf_size, leaf_basis, leaf_transfer, mid_transfer, leaf_parent, send_leaf, pair_leaf,
    leaf_coupling, send_mid, pair_mid, mid_coupling, top_pairs, top_coupling,
):
    rank = leaf_basis.shape[1]
    ports = charges.shape[1]
    mids = mid_transfer.shape[0]
    slots = send_mid.shape[0]
    groups, per_cluster = lax.axis_size("group"), lax.axis_size("cluster")
    owners = groups * per_cluster
    lines = per_cluster // 2
    per_pair = slots // owners
    group, lane = lax.axis_index("group"), lax.axis_index("cluster")

    group_at, lane_at = group.astype(jnp.int32)[None], lane.astype(jnp.int32)[None]
    coef, lifted, *own_messages = up_sweep(
        (per_cluster, per_pair), groups, group_at, lane_at, charges, leaf_size, leaf_basis,
        leaf_transfer, mid_transfer, leaf_parent, send_mid,
    )
    up_rows = lifted.shape[0]
    outgoing = spread(send_leaf, coef)

    received = [lifted] * lines
    for d in range(lines - 1, 0, -1):
        received[d] = lax.ppermute(lifted, "cluster", [(c, c ^ (2 * d)) for c in range(per_cluster)])
    wide, basis_t, mid_wide = prepare(
        lifted, leaf_coupling, leaf_basis, leaf_transfer, mid_coupling, mid_transfer
    )

    def spot_of(sender):
        at_group, at_lane = sender // per_cluster, sender % per_cluster
        line = (at_lane // 2) ^ (lane // 2)
        return ((at_group ^ group) * 2 + ((at_lane ^ lane) & 1)) * lines + line

    spot = spot_of(pair_mid // per_pair) * per_pair + pair_mid % per_pair
    spot = jnp.where((pair_mid >= 0) & (pair_mid < slots), spot, slots)
    wanted = lax.dynamic_slice_in_dim(top_pairs, lane, 1, 0)[0]
    tops = jnp.where((wanted >= 0) & (wanted < owners), spot_of(wanted), owners)

    own_messages, received[-1] = lax.optimization_barrier((own_messages, received[-1]))
    bounds = (0, 1, lines)
    swap = [(c, c ^ 1) for c in range(per_cluster)]
    near_side, far_side = [], []
    for low, high in zip(bounds[:-1], bounds[1:]):
        sizes = (high - low, per_cluster, up_rows, mids, rank, per_pair, groups)
        messages = own_messages if low == 0 else select(sizes, group_at, lane_at, received[low:high])
        moved = [messages[0]]
        for d in range(1, groups):
            moved.append(lax.ppermute(messages[d], "group", [(g, g ^ d) for g in range(groups)]))
        if high < lines:
            near_side += moved
        if low == 0:
            outgoing, near_side, received[1:] = lax.optimization_barrier(
                (outgoing, near_side, received[1:])
            )
            arrived = lax.all_to_all(outgoing, AXES, split_axis=0, concat_axis=0, tiled=True)
            far_side = [lax.ppermute(m, "cluster", swap) for m in near_side]
        if high == lines:
            ready = (moved, far_side, mid_wide, spot, tops, pair_leaf)
            moved, far_side, mid_wide, spot, tops, pair_leaf = lax.optimization_barrier(ready)
            near_side += moved
            far_side += [lax.ppermute(m, "cluster", swap) for m in moved]

    return tail(
        bounds, per_pair, groups, leaf_parent, spot, lane_at, tops, leaf_size, pair_leaf, near_side,
        far_side, arrived, mid_wide, top_coupling, wide, basis_t,
    )


def solution(mesh):
    both = P(AXES)
    in_specs = (
        P(AXES, None),
        both,
        P(AXES, None, None),
        P(AXES, None, None),
        P(AXES, None, None),
        both,
        both,
        P(AXES, None),
        P(AXES, None, None),
        both,
        P(AXES, None),
        P(AXES, None, None),
        P("group", None),
        P("group", None, None),
    )
    return jax.shard_map(
        body, mesh=mesh, in_specs=in_specs, out_specs=P(AXES, None), check_vma=False
    )
```

profile of v0, /device:TPU:0, one launch (start us, length us, event | category | flops | bytes accessed | tf_op | source)
XLA Modules:
  0.0 108.0 jit_solution(16712704375174066523)
XLA Ops:
  0.0 7.4 %up_sweep.1 = (f32[32,64,128]{2,1,0:T(8,128)}, f32[584,128]{1,0:T(8,128)}, f32[5,64,128]{2,1,0:T(8,128)}, f32[5,64,128]{2,1,0:T(8,128)}, f32[5,64,128]{2,1,0:T(8,128)}, /*index=5*/f32[5,64,128]{2,1,0:T(8,128)}) custom-call(s32[32]{0:T(128)} %size.3, s32[32]{0:T(128)} %parent.3, s32[64]{0:T(128)} %slots.1, s32[1]{0:T(128)} %bitcast.group_at, ...), custom_call_target="tpu_custom_call" | custom-call | flops 1000000000 | bytes 10000000 | tf_op jit(solution)/shard_map/up_sweep/pallas_call | solution.py:120
  7.4 5.1 %collective-permute-start = (f32[584,128]{1,0:T(8,128)}, f32[584,128]{1,0:T(8,128)S(1)}, u32[]{:S(2)}, u32[]{:S(2)}) collective-permute-start(f32[584,128]{1,0:T(8,128)} %get-tuple-element.48.after), channel_id=1, source_target_pairs={{0,6},{1,7},{2,4},{3,5},{4,2},{5,3},{6,0},{7,1},{8,14},{9,15},{10,... | collective-permute-start | bytes 897032 | tf_op jit(solution)/shard_map/ppermute | solution.py:457
  12.5 0.0 collective-permute-start.5
  12.5 0.6 collective-permute-start.4
  13.2 7.6 %collective-permute-done.refs_2_ = f32[584,128]{1,0:T(8,128)S(1)} collective-permute-done((f32[584,128]{1,0:T(8,128)}, f32[584,128]{1,0:T(8,128)S(1)}, u32[]{:S(2)}, u32[]{:S(2)}) %collective-permute-start) | collective-permute-done | bytes 299040 | tf_op jit(solution)/shard_map/ppermute | solution.py:457
  20.8 1.7 %collective-permute-start.1 = (f32[5,64,128]{2,1,0:T(8,128)}, f32[5,64,128]{2,1,0:T(8,128)S(1)}, u32[]{:S(2)}, u32[]{:S(2)}) collective-permute-start(f32[5,64,128]{2,1,0:T(8,128)} %get-tuple-element.50), channel_id=1, source_target_pairs={{0,8},{8,0},{16,24},{24,16},{1,9},{9,1},{17,25},{25,17},{2,10},{10... | collective-permute-start | bytes 491528 | tf_op jit(solution)/shard_map/ppermute | solution.py:481
  22.5 1.5 %collective-permute-start.2 = (f32[5,64,128]{2,1,0:T(8,128)}, f32[5,64,128]{2,1,0:T(8,128)S(1)}, u32[]{:S(2)}, u32[]{:S(2)}) collective-permute-start(f32[5,64,128]{2,1,0:T(8,128)} %get-tuple-element.51), channel_id=1, source_target_pairs={{0,16},{8,24},{16,0},{24,8},{1,17},{9,25},{17,1},{25,9},{2,18},{10... | collective-permute-start | bytes 491528 | tf_op jit(solution)/shard_map/ppermute | solution.py:481
  24.0 0.3 collective-permute-start.3
  24.3 2.7 %spread.1 = f32[64,64,128]{2,1,0:T(8,128)} custom-call(s32[64]{0:T(128)} %send.1, f32[32,64,128]{2,1,0:T(8,128)} %get-tuple-element.43.coef), custom_call_target="tpu_custom_call" | custom-call | bytes 4000000 | tf_op jit(solution)/shard_map/spread/pallas_call | solution.py:158
  27.0 11.2 %collective-permute-done.5.refs_1_ = f32[584,128]{1,0:T(8,128)S(1)} collective-permute-done((f32[584,128]{1,0:T(8,128)}, f32[584,128]{1,0:T(8,128)S(1)}, u32[]{:S(2)}, u32[]{:S(2)}) %collective-permute-start.5) | collective-permute-done | bytes 299040 | tf_op jit(solution)/shard_map/ppermute | solution.py:457
  38.2 0.0 collective-permute-done.4.refs_0_
  38.2 0.0 collective-permute-done.1.refs_1_
  38.2 0.0 copy-start.9
  38.2 0.0 collective-permute-done.2.refs_2_
  38.2 0.0 collective-permute-done.3.refs_3_
  38.3 6.6 %all-to-all-start = ((f32[64,64,128]{2,1,0:T(8,128)}), f32[64,64,128]{2,1,0:T(8,128)S(1)}, u32[]{:S(2)}, u32[]{:S(2)}) async-start(f32[64,64,128]{2,1,0:T(8,128)} %spread.1), calls=%async_computation | async-start | bytes 4194304 | tf_op jit(solution)/shard_map/all_to_all | solution.py:488
  44.9 2.7 %select.31 = (f32[15,64,128]{2,1,0:T(8,128)}, f32[15,64,128]{2,1,0:T(8,128)}, f32[15,64,128]{2,1,0:T(8,128)}, f32[15,64,128]{2,1,0:T(8,128)}) custom-call(s32[1]{0:T(128)} %bitcast.group_at, s32[1]{0:T(128)} %bitcast.1.lane_at.position, f32[584,128]{1,0:T(8,128)} %copy-done.7, f32[584,128]{1,0:T(8,128)} %copy-done.6, f32[584,128]{1,0:T(8,128)} %copy-done.5), custom_call_target="tpu_custom_call" | custom-call | bytes 4000000 | tf_op jit(solution)/shard_map/select/pallas_call | solution.py:208
  47.6 1.8 %collective-permute-start.6 = (f32[15,64,128]{2,1,0:T(8,128)}, f32[15,64,128]{2,1,0:T(8,128)S(1)}, u32[]{:S(2)}, u32[]{:S(2)}) collective-permute-start(f32[15,64,128]{2,1,0:T(8,128)} %get-tuple-element.58), channel_id=1, source_target_pairs={{0,8},{8,0},{16,24},{24,16},{1,9},{9,1},{17,25},{25,17},{2,10},{10... | collective-permute-start | bytes 1474568 | tf_op jit(solution)/shard_map/ppermute | solution.py:481
  49.5 1.5 %collective-permute-start.7 = (f32[15,64,128]{2,1,0:T(8,128)}, f32[15,64,128]{2,1,0:T(8,128)}, u32[]{:S(2)}, u32[]{:S(2)}) collective-permute-start(f32[15,64,128]{2,1,0:T(8,128)} %get-tuple-element.59), channel_id=1, source_target_pairs={{0,16},{8,24},{16,0},{24,8},{1,17},{9,25},{17,1},{25,9},{2,18},{10... | collective-permute-start | bytes 1474568 | tf_op jit(solution)/shard_map/ppermute | solution.py:481
  50.9 0.3 collective-permute-start.8
  51.2 0.2 dynamic-slice_reduce_fusion
  51.4 0.0 copy-start.17
  51.4 0.0 copy-start.16
  51.4 0.0 copy-start.1
  51.4 0.0 copy-start.2
  51.5 12.3 %prepare.1 = (bf16[32,128,832]{2,1,0:T(8,128)(2,1)}, bf16[32,256,128]{2,1,0:T(8,128)(2,1)}, bf16[8,128,2112]{2,1,0:T(8,128)(2,1)}) custom-call(f32[584,128]{1,0:T(8,128)} %get-tuple-element.48.after, f32[32,64,768]{2,1,0:T(8,128)} %coupling.1, f32[32,64,256]{2,1,0:T(8,128)} %basis.3, f32[32,64,64]{2,1,0:T(8,128)} %transfer.3, f32[8,64,2048]{2,1,0:T(8,128)} %mid_coupling.1, ...), custom_call_target="tpu_custom_call" | custom-call | bytes 30000000 | tf_op jit(solution)/shard_map/prepare/pallas_call | solution.py:245
  63.8 0.0 collective-permute-start.9
  63.8 0.5 collective-permute-start.10
  64.3 0.8 collective-permute-done.9.refs_8_
  65.2 0.1 collective-permute-start.11
  65.3 0.1 collective-permute-done.10.refs_9_
  65.4 0.3 collective-permute-start.12
  65.7 0.9 collective-permute-done.11.refs_10_
  66.6 0.4 collective-permute-done.12.refs_11_
  67.0 8.3 %collective-permute-done.6.refs_5_ = f32[15,64,128]{2,1,0:T(8,128)S(1)} collective-permute-done((f32[15,64,128]{2,1,0:T(8,128)}, f32[15,64,128]{2,1,0:T(8,128)S(1)}, u32[]{:S(2)}, u32[]{:S(2)}) %collective-permute-start.6) | collective-permute-done | bytes 491552 | tf_op jit(solution)/shard_map/ppermute | solution.py:481
  75.4 3.1 %collective-permute-done.7.refs_6_ = f32[15,64,128]{2,1,0:T(8,128)} collective-permute-done((f32[15,64,128]{2,1,0:T(8,128)}, f32[15,64,128]{2,1,0:T(8,128)}, u32[]{:S(2)}, u32[]{:S(2)}) %collective-permute-start.7) | collective-permute-done | bytes 491552 | tf_op jit(solution)/shard_map/ppermute | solution.py:481
  78.5 12.2 %collective-permute-done.8.refs_7_ = f32[15,64,128]{2,1,0:T(8,128)} collective-permute-done((f32[15,64,128]{2,1,0:T(8,128)}, f32[15,64,128]{2,1,0:T(8,128)}, u32[]{:S(2)}, u32[]{:S(2)}) %collective-permute-start.8) | collective-permute-done | bytes 491552 | tf_op jit(solution)/shard_map/ppermute | solution.py:481
  90.6 0.0 collective-permute-start.13
  90.6 0.5 collective-permute-start.14
  91.2 0.0 collective-permute-start.15
  91.2 0.5 collective-permute-start.16
  91.7 0.1 copy.15.pair_leaf
  91.8 0.9 collective-permute-done.13.refs_12_
  92.6 1.4 %collective-permute-done.14.refs_13_ = f32[15,64,128]{2,1,0:T(8,128)} collective-permute-done((f32[15,64,128]{2,1,0:T(8,128)S(1)}, f32[15,64,128]{2,1,0:T(8,128)}, u32[]{:S(2)}, u32[]{:S(2)}) %collective-permute-start.14) | collective-permute-done | bytes 491552 | tf_op jit(solution)/shard_map/ppermute | solution.py:494
  94.0 0.2 collective-permute-done.15.refs_14_
  94.3 0.7 collective-permute-done.16.refs_15_
  95.0 0.0 all-to-all-done.refs_16_
  95.0 13.0 %tail.1 = f32[8192,128]{1,0:T(8,128)} custom-call(s32[32]{0:T(128)S(1)} %copy-done.1, s32[8,32]{1,0:T(8,128)S(1)} %fusion.7.pair, s32[1]{0:T(128)} %bitcast.1.lane_at.position, s32[4]{0:T(128)S(1)} %and_select_fusion.3.tops, s32[32]{0:T(128)S(1)} %copy-done.2, s32[32,12]{1,0:T(8,128)S(1)} %copy.15.pair_leaf, f32[5,64,128]{2,1,0:T(8,128)} %get-tuple-element.61.refs_0_, ...), custom_call_target="tpu_custom_call" | custom-call | flops 6000000000 | bytes 20000000 | tf_op jit(solution)/shard_map/tail/pallas_call | solution.py:419
  (33 shorter events, 0.1 us)
Async XLA Ops:
  0.0 51.2 %copy-start = (s32[8,4]{0,1:T(4,128)S(1)}, s32[8,4]{0,1:T(4,128)}, u32[]{:S(2)}) copy-start(s32[8,4]{0,1:T(4,128)} %param.26) | copy-start | bytes 388
  7.4 13.4 %collective-permute-start = (f32[584,128]{1,0:T(8,128)}, f32[584,128]{1,0:T(8,128)S(1)}, u32[]{:S(2)}, u32[]{:S(2)}) collective-permute-start(f32[584,128]{1,0:T(8,128)} %get-tuple-element.48.after), channel_id=1, source_target_pairs={{0,6},{1,7},{2,4},{3,5},{4,2},{5,3},{6,0},{7,1},{8,14},{9,15},{10,... | collective-permute-start | bytes 897032 | tf_op jit(solution)/shard_map/ppermute | solution.py:457
  12.5 25.7 %collective-permute-start.5 = (f32[584,128]{1,0:T(8,128)}, f32[584,128]{1,0:T(8,128)S(1)}, u32[]{:S(2)}, u32[]{:S(2)}) collective-permute-start(f32[584,128]{1,0:T(8,128)} %get-tuple-element.48.after), channel_id=1, source_target_pairs={{0,4},{1,5},{2,6},{3,7},{4,0},{5,1},{6,2},{7,3},{8,12},{9,13},{10,... | collective-permute-start | bytes 897032 | tf_op jit(solution)/shard_map/ppermute | solution.py:457
  12.5 25.7 %collective-permute-start.4 = (f32[584,128]{1,0:T(8,128)}, f32[584,128]{1,0:T(8,128)S(1)}, u32[]{:S(2)}, u32[]{:S(2)}) collective-permute-start(f32[584,128]{1,0:T(8,128)} %get-tuple-element.48.after), channel_id=1, source_target_pairs={{0,2},{1,3},{2,0},{3,1},{4,6},{5,7},{6,4},{7,5},{8,10},{9,11},{10,... | collective-permute-start | bytes 897032 | tf_op jit(solution)/shard_map/ppermute | solution.py:457
  20.8 24.1 %copy-start.5 = (f32[584,128]{1,0:T(8,128)}, f32[584,128]{1,0:T(8,128)S(1)}, u32[]{:S(2)}) copy-start(f32[584,128]{1,0:T(8,128)S(1)} %collective-permute-done.refs_2_) | copy-start | bytes 897028
  20.8 17.4 %collective-permute-start.1 = (f32[5,64,128]{2,1,0:T(8,128)}, f32[5,64,128]{2,1,0:T(8,128)S(1)}, u32[]{:S(2)}, u32[]{:S(2)}) collective-permute-start(f32[5,64,128]{2,1,0:T(8,128)} %get-tuple-element.50), channel_id=1, source_target_pairs={{0,8},{8,0},{16,24},{24,16},{1,9},{9,1},{17,25},{25,17},{2,10},{10... | collective-permute-start | bytes 491528 | tf_op jit(solution)/shard_map/ppermute | solution.py:481
  22.5 15.7 %collective-permute-start.2 = (f32[5,64,128]{2,1,0:T(8,128)}, f32[5,64,128]{2,1,0:T(8,128)S(1)}, u32[]{:S(2)}, u32[]{:S(2)}) collective-permute-start(f32[5,64,128]{2,1,0:T(8,128)} %get-tuple-element.51), channel_id=1, source_target_pairs={{0,16},{8,24},{16,0},{24,8},{1,17},{9,25},{17,1},{25,9},{2,18},{10... | collective-permute-start | bytes 491528 | tf_op jit(solution)/shard_map/ppermute | solution.py:481
  24.0 14.2 %collective-permute-start.3 = (f32[5,64,128]{2,1,0:T(8,128)}, f32[5,64,128]{2,1,0:T(8,128)}, u32[]{:S(2)}, u32[]{:S(2)}) collective-permute-start(f32[5,64,128]{2,1,0:T(8,128)} %get-tuple-element.52), channel_id=1, source_target_pairs={{0,24},{8,16},{16,8},{24,0},{1,25},{9,17},{17,9},{25,1},{2,26},{10... | collective-permute-start | bytes 491528 | tf_op jit(solution)/shard_map/ppermute | solution.py:481
  38.2 6.7 %copy-start.6 = (f32[584,128]{1,0:T(8,128)}, f32[584,128]{1,0:T(8,128)S(1)}, u32[]{:S(2)}) copy-start(f32[584,128]{1,0:T(8,128)S(1)} %collective-permute-done.5.refs_1_) | copy-start | bytes 897028
  38.2 6.7 %copy-start.7 = (f32[584,128]{1,0:T(8,128)}, f32[584,128]{1,0:T(8,128)S(1)}, u32[]{:S(2)}) copy-start(f32[584,128]{1,0:T(8,128)S(1)} %collective-permute-done.4.refs_0_) | copy-start | bytes 897028
  38.2 25.6 %copy-start.9 = (f32[5,64,128]{2,1,0:T(8,128)}, f32[5,64,128]{2,1,0:T(8,128)S(1)}, u32[]{:S(2)}) copy-start(f32[5,64,128]{2,1,0:T(8,128)S(1)} %collective-permute-done.1.refs_1_) | copy-start | bytes 491524
  38.2 9.4 %copy-start.10 = (f32[5,64,128]{2,1,0:T(8,128)}, f32[5,64,128]{2,1,0:T(8,128)S(1)}, u32[]{:S(2)}) copy-start(f32[5,64,128]{2,1,0:T(8,128)S(1)} %collective-permute-done.2.refs_2_) | copy-start | bytes 491524
  38.3 56.7 %all-to-all-start = ((f32[64,64,128]{2,1,0:T(8,128)}), f32[64,64,128]{2,1,0:T(8,128)S(1)}, u32[]{:S(2)}, u32[]{:S(2)}) async-start(f32[64,64,128]{2,1,0:T(8,128)} %spread.1), calls=%async_computation | async-start | bytes 4194304 | tf_op jit(solution)/shard_map/all_to_all | solution.py:488
  47.6 27.7 %collective-permute-start.6 = (f32[15,64,128]{2,1,0:T(8,128)}, f32[15,64,128]{2,1,0:T(8,128)S(1)}, u32[]{:S(2)}, u32[]{:S(2)}) collective-permute-start(f32[15,64,128]{2,1,0:T(8,128)} %get-tuple-element.58), channel_id=1, source_target_pairs={{0,8},{8,0},{16,24},{24,16},{1,9},{9,1},{17,25},{25,17},{2,10},{10... | collective-permute-start | bytes 1474568 | tf_op jit(solution)/shard_map/ppermute | solution.py:481
  49.5 29.0 %collective-permute-start.7 = (f32[15,64,128]{2,1,0:T(8,128)}, f32[15,64,128]{2,1,0:T(8,128)}, u32[]{:S(2)}, u32[]{:S(2)}) collective-permute-start(f32[15,64,128]{2,1,0:T(8,128)} %get-tuple-element.59), channel_id=1, source_target_pairs={{0,16},{8,24},{16,0},{24,8},{1,17},{9,25},{17,1},{25,9},{2,18},{10... | collective-permute-start | bytes 1474568 | tf_op jit(solution)/shard_map/ppermute | solution.py:481
  50.9 39.7 %collective-permute-start.8 = (f32[15,64,128]{2,1,0:T(8,128)}, f32[15,64,128]{2,1,0:T(8,128)}, u32[]{:S(2)}, u32[]{:S(2)}) collective-permute-start(f32[15,64,128]{2,1,0:T(8,128)} %get-tuple-element.60), channel_id=1, source_target_pairs={{0,24},{8,16},{16,8},{24,0},{1,25},{9,17},{17,9},{25,1},{2,26},{10... | collective-permute-start | bytes 1474568 | tf_op jit(solution)/shard_map/ppermute | solution.py:481
  51.4 12.4 %copy-start.8 = (f32[5,64,128]{2,1,0:T(8,128)S(1)}, f32[5,64,128]{2,1,0:T(8,128)}, u32[]{:S(2)}) copy-start(f32[5,64,128]{2,1,0:T(8,128)} %get-tuple-element.61.refs_0_) | copy-start | bytes 491524
  51.4 12.9 %copy-start.17 = (s32[8,32]{1,0:T(8,128)S(1)}, s32[8,32]{1,0:T(8,128)}, u32[]{:S(2)}) copy-start(s32[8,32]{1,0:T(8,128)} %param.24) | copy-start | bytes 3076
  51.4 13.8 %copy-start.11 = (f32[5,64,128]{2,1,0:T(8,128)S(1)}, f32[5,64,128]{2,1,0:T(8,128)}, u32[]{:S(2)}) copy-start(f32[5,64,128]{2,1,0:T(8,128)} %copy-done.10) | copy-start | bytes 491524
  51.4 39.2 %copy-start.3 = (f32[15,64,128]{2,1,0:T(8,128)S(1)}, f32[15,64,128]{2,1,0:T(8,128)}, u32[]{:S(2)}) copy-start(f32[15,64,128]{2,1,0:T(8,128)} %get-tuple-element.69.refs_4_) | copy-start | bytes 1474564
  51.4 40.3 %copy-start.16 = (s32[32,12]{0,1:T(8,128)S(1)}, s32[32,12]{0,1:T(8,128)}, u32[]{:S(2)}) copy-start(s32[32,12]{0,1:T(8,128)} %param.21) | copy-start | bytes 4612
  51.4 43.6 %copy-start.1 = (s32[32]{0:T(128)S(1)}, s32[32]{0:T(128)}, u32[]{:S(2)}) copy-start(s32[32]{0:T(128)} %parent.3) | copy-start | bytes 388
  51.4 43.6 %copy-start.2 = (s32[32]{0:T(128)S(1)}, s32[32]{0:T(128)}, u32[]{:S(2)}) copy-start(s32[32]{0:T(128)} %size.3) | copy-start | bytes 388
  63.8 1.4 %collective-permute-start.9 = (f32[5,64,128]{2,1,0:T(8,128)S(1)}, f32[5,64,128]{2,1,0:T(8,128)S(1)}, u32[]{:S(2)}, u32[]{:S(2)}) collective-permute-start(f32[5,64,128]{2,1,0:T(8,128)S(1)} %copy-done.8), channel_id=1, source_target_pairs={{0,1},{1,0},{2,3},{3,2},{4,5},{5,4},{6,7},{7,6},{8,9},{9,8},{10,11... | collective-permute-start | bytes 491528 | tf_op jit(solution)/shard_map/ppermute | solution.py:489
  63.8 1.6 %collective-permute-start.10 = (f32[5,64,128]{2,1,0:T(8,128)S(1)}, f32[5,64,128]{2,1,0:T(8,128)S(1)}, u32[]{:S(2)}, u32[]{:S(2)}) collective-permute-start(f32[5,64,128]{2,1,0:T(8,128)S(1)} %collective-permute-done.1.refs_1_), channel_id=1, source_target_pairs={{0,1},{1,0},{2,3},{3,2},{4,5},{5,4},{6,7},{7,6},{8,9},{9,8},{10,11... | collective-permute-start | bytes 491528 | tf_op jit(solution)/shard_map/ppermute | solution.py:489
  65.2 26.0 %copy-start.12 = (f32[5,64,128]{2,1,0:T(8,128)}, f32[5,64,128]{2,1,0:T(8,128)S(1)}, u32[]{:S(2)}) copy-start(f32[5,64,128]{2,1,0:T(8,128)S(1)} %collective-permute-done.9.refs_8_) | copy-start | bytes 491524
  65.2 1.4 %collective-permute-start.11 = (f32[5,64,128]{2,1,0:T(8,128)S(1)}, f32[5,64,128]{2,1,0:T(8,128)S(1)}, u32[]{:S(2)}, u32[]{:S(2)}) collective-permute-start(f32[5,64,128]{2,1,0:T(8,128)S(1)} %copy-done.11), channel_id=1, source_target_pairs={{0,1},{1,0},{2,3},{3,2},{4,5},{5,4},{6,7},{7,6},{8,9},{9,8},{10,11... | collective-permute-start | bytes 491528 | tf_op jit(solution)/shard_map/ppermute | solution.py:489
  65.4 25.7 %copy-start.13 = (f32[5,64,128]{2,1,0:T(8,128)}, f32[5,64,128]{2,1,0:T(8,128)S(1)}, u32[]{:S(2)}) copy-start(f32[5,64,128]{2,1,0:T(8,128)S(1)} %collective-permute-done.10.refs_9_) | copy-start | bytes 491524
  65.4 1.6 %collective-permute-start.12 = (f32[5,64,128]{2,1,0:T(8,128)}, f32[5,64,128]{2,1,0:T(8,128)S(1)}, u32[]{:S(2)}, u32[]{:S(2)}) collective-permute-start(f32[5,64,128]{2,1,0:T(8,128)} %collective-permute-done.3.refs_3_), channel_id=1, source_target_pairs={{0,1},{1,0},{2,3},{3,2},{4,5},{5,4},{6,7},{7,6},{8,9},{9,8},{10,11... | collective-permute-start | bytes 491528 | tf_op jit(solution)/shard_map/ppermute | solution.py:489
  66.6 28.4 %copy-start.14 = (f32[5,64,128]{2,1,0:T(8,128)}, f32[5,64,128]{2,1,0:T(8,128)S(1)}, u32[]{:S(2)}) copy-start(f32[5,64,128]{2,1,0:T(8,128)S(1)} %collective-permute-done.11.refs_10_) | copy-start | bytes 491524
  67.0 28.0 %copy-start.15 = (f32[5,64,128]{2,1,0:T(8,128)}, f32[5,64,128]{2,1,0:T(8,128)S(1)}, u32[]{:S(2)}) copy-start(f32[5,64,128]{2,1,0:T(8,128)S(1)} %collective-permute-done.12.refs_11_) | copy-start | bytes 491524
  75.4 19.6 %copy-start.4 = (f32[15,64,128]{2,1,0:T(8,128)}, f32[15,64,128]{2,1,0:T(8,128)S(1)}, u32[]{:S(2)}) copy-start(f32[15,64,128]{2,1,0:T(8,128)S(1)} %collective-permute-done.6.refs_5_) | copy-start | bytes 1474564
  90.6 2.0 %collective-permute-start.13 = (f32[15,64,128]{2,1,0:T(8,128)S(1)}, f32[15,64,128]{2,1,0:T(8,128)}, u32[]{:S(2)}, u32[]{:S(2)}) collective-permute-start(f32[15,64,128]{2,1,0:T(8,128)S(1)} %copy-done.3), channel_id=1, source_target_pairs={{0,1},{1,0},{2,3},{3,2},{4,5},{5,4},{6,7},{7,6},{8,9},{9,8},{10,11... | collective-permute-start | bytes 1474568 | tf_op jit(solution)/shard_map/ppermute | solution.py:494
  90.6 3.4 %collective-permute-start.14 = (f32[15,64,128]{2,1,0:T(8,128)S(1)}, f32[15,64,128]{2,1,0:T(8,128)}, u32[]{:S(2)}, u32[]{:S(2)}) collective-permute-start(f32[15,64,128]{2,1,0:T(8,128)S(1)} %collective-permute-done.6.refs_5_), channel_id=1, source_target_pairs={{0,1},{1,0},{2,3},{3,2},{4,5},{5,4},{6,7},{7,6},{8,9},{9,8},{10,11... | collective-permute-start | bytes 1474568 | tf_op jit(solution)/shard_map/ppermute | solution.py:494
  91.2 3.1 %collective-permute-start.15 = (f32[15,64,128]{2,1,0:T(8,128)}, f32[15,64,128]{2,1,0:T(8,128)}, u32[]{:S(2)}, u32[]{:S(2)}) collective-permute-start(f32[15,64,128]{2,1,0:T(8,128)} %collective-permute-done.7.refs_6_), channel_id=1, source_target_pairs={{0,1},{1,0},{2,3},{3,2},{4,5},{5,4},{6,7},{7,6},{8,9},{9,8},{10,11... | collective-permute-start | bytes 1474568 | tf_op jit(solution)/shard_map/ppermute | solution.py:494
  91.2 3.8 %collective-permute-start.16 = (f32[15,64,128]{2,1,0:T(8,128)}, f32[15,64,128]{2,1,0:T(8,128)}, u32[]{:S(2)}, u32[]{:S(2)}) collective-permute-start(f32[15,64,128]{2,1,0:T(8,128)} %collective-permute-done.8.refs_7_), channel_id=1, source_target_pairs={{0,1},{1,0},{2,3},{3,2},{4,5},{5,4},{6,7},{7,6},{8,9},{9,8},{10,11... | collective-permute-start | bytes 1474568 | tf_op jit(solution)/shard_map/ppermute | solution.py:494
where the time goes:
time: 110 us; the launch traced here: 108 us
  waiting for transfers between devices  47.9 us (44%)
  Pallas kernels  38.2 us (35%)
  starting transfers between devices  21.3 us (19%)
    ppermute x6, waiting for transfers between devices, body(): lax.ppermute(messages[d], 'group', [(g, g ^ d) for g in range(groups)])  23.6 us
    ppermute x3, waiting for transfers between devices, body(): lax.ppermute(lifted, 'cluster', [(c, c ^ 2 * d) for c in range(per_cluste...  18.8 us
    pallas_call x1, Pallas kernels, tail(): pl.pallas_call(functools.partial(tail_kernel, (bounds, per_pair, groups,...  13 us
    pallas_call x1, Pallas kernels, prepare(): pl.pallas_call(prepare_kernel, grid=(steps,), in_specs=[pl.BlockSpec(memo...  12.3 us
    pallas_call x1, Pallas kernels, up_sweep(): pl.pallas_call(functools.partial(up_kernel, sizes), grid_spec=pltpu.Prefe...  7.41 us
    ppermute x6, starting transfers between devices, body(): lax.ppermute(messages[d], 'group', [(g, g ^ d) for g in range(groups)])  7.04 us
    all_to_all x1, starting transfers between devices, body(): lax.all_to_all(outgoing, AXES, split_axis=0, concat_axis=0, tiled=True)  6.59 us
    ppermute x3, starting transfers between devices, body(): lax.ppermute(lifted, 'cluster', [(c, c ^ 2 * d) for c in range(per_cluste...  5.74 us
  transfers between devices with their start and end apart: 18, of which 13 were waited for; matrix products, arithmetic and copies ran while one was open for 0% of the time, Pallas kernels for 16%

commit v1 on v0

--- a/solution.py
+++ b/solution.py
@@ -453,7 +453,7 @@
     outgoing = spread(send_leaf, coef)
 
     received = [lifted] * lines
-    for d in range(lines - 1, 0, -1):
+    for d in range(1, lines):
         received[d] = lax.ppermute(lifted, "cluster", [(c, c ^ (2 * d)) for c in range(per_cluster)])
     wide, basis_t, mid_wide = prepare(
         lifted, leaf_coupling, leaf_basis, leaf_transfer, mid_coupling, mid_transfer
@@ -469,7 +469,7 @@
     wanted = lax.dynamic_slice_in_dim(top_pairs, lane, 1, 0)[0]
     tops = jnp.where((wanted >= 0) & (wanted < owners), spot_of(wanted), owners)
 
-    own_messages, received[-1] = lax.optimization_barrier((own_messages, received[-1]))
+    own_messages, received[1] = lax.optimization_barrier((own_messages, received[1]))
     bounds = (0, 1, lines)
     swap = [(c, c ^ 1) for c in range(per_cluster)]
     near_side, far_side = [], []
@@ -488,8 +488,8 @@
             arrived = lax.all_to_all(outgoing, AXES, split_axis=0, concat_axis=0, tiled=True)
             far_side = [lax.ppermute(m, "cluster", swap) for m in near_side]
         if high == lines:
-            ready = (moved, far_side, mid_wide, spot, tops, pair_leaf)
-            moved, far_side, mid_wide, spot, tops, pair_leaf = lax.optimization_barrier(ready)
+            ready = (moved[1], far_side, mid_wide, spot, tops, pair_leaf)
+            moved[1], far_side, mid_wide, spot, tops, pair_leaf = lax.optimization_barrier(ready)
             near_side += moved
             far_side += [lax.ppermute(m, "cluster", swap) for m in moved]
 

time: 110 us -> 108 us (0.982); the launches traced: 108 us -> 107 us
  starting transfers between devices: 21.3 us -> 19.2 us
  waiting for transfers between devices: 47.9 us -> 49.5 us
    all_to_all x1, starting transfers between devices: 6.59 us -> 4.86 us  [body(): lax.all_to_all(outgoing, AXES, split_axis=0, concat_axis=0, tiled=True)]
    all_to_all x1, waiting for transfers between devices: 0.03 us -> 1.65 us  [body(): lax.all_to_all(outgoing, AXES, split_axis=0, concat_axis=0, tiled=True)]
    ppermute x3, waiting for transfers between devices: 18.8 us -> 20 us  [body(): lax.ppermute(lifted, 'cluster', [(c, c ^ 2 * d) for c in range(per_cluste...]
    ppermute x4, waiting for transfers between devices: 3.2 us -> 2.09 us  [body(): far_side += [lax.ppermute(m, 'cluster', swap) for m in moved]]
  transfers between devices with their start and end apart: 18 -> 18, of which waited for: 13 -> 13; matrix products, arithmetic and copies ran while one was open for 0% -> 0% of each run, Pallas kernels for 16% -> 17%
where the time goes in v1:
time: 108 us; the launch traced here: 107 us
  waiting for transfers between devices  49.5 us (46%)
  Pallas kernels  38.2 us (35%)
  starting transfers between devices  19.2 us (18%)
    ppermute x6, waiting for transfers between devices, body(): lax.ppermute(messages[d], 'group', [(g, g ^ d) for g in range(groups)])  23.6 us
    ppermute x3, waiting for transfers between devices, body(): lax.ppermute(lifted, 'cluster', [(c, c ^ 2 * d) for c in range(per_cluste...  20 us
    pallas_call x1, Pallas kernels, tail(): pl.pallas_call(functools.partial(tail_kernel, (bounds, per_pair, groups,...  13 us
    pallas_call x1, Pallas kernels, prepare(): pl.pallas_call(prepare_kernel, grid=(steps,), in_specs=[pl.BlockSpec(memo...  12.3 us
    pallas_call x1, Pallas kernels, up_sweep(): pl.pallas_call(functools.partial(up_kernel, sizes), grid_spec=pltpu.Prefe...  7.43 us
    ppermute x6, starting transfers between devices, body(): lax.ppermute(messages[d], 'group', [(g, g ^ d) for g in range(groups)])  7.04 us
    ppermute x3, starting transfers between devices, body(): lax.ppermute(lifted, 'cluster', [(c, c ^ 2 * d) for c in range(per_cluste...  5.66 us
    all_to_all x1, starting transfers between devices, body(): lax.all_to_all(outgoing, AXES, split_axis=0, concat_axis=0, tiled=True)  4.86 us
  transfers between devices with their start and end apart: 18, of which 13 were waited for; matrix products, arithmetic and copies ran while one was open for 0% of the time, Pallas kernels for 17%

profile of v1, /device:TPU:0, one launch (start us, length us, event | category | flops | bytes accessed | tf_op | source)
XLA Modules:
  0.0 107.4 jit_solution(12528799333639276879)
XLA Ops:
  0.0 7.4 %up_sweep.1 = (f32[32,64,128]{2,1,0:T(8,128)}, f32[584,128]{1,0:T(8,128)}, f32[5,64,128]{2,1,0:T(8,128)}, f32[5,64,128]{2,1,0:T(8,128)}, f32[5,64,128]{2,1,0:T(8,128)}, /*index=5*/f32[5,64,128]{2,1,0:T(8,128)}) custom-call(s32[32]{0:T(128)} %size.3, s32[32]{0:T(128)} %parent.3, s32[64]{0:T(128)} %slots.1, s32[1]{0:T(128)} %bitcast.group_at, ...), custom_call_target="tpu_custom_call" | custom-call | flops 1000000000 | bytes 10000000 | tf_op jit(solution)/shard_map/up_sweep/pallas_call | solution.py:120
  7.4 3.1 %collective-permute-start = (f32[584,128]{1,0:T(8,128)}, f32[584,128]{1,0:T(8,128)S(1)}, u32[]{:S(2)}, u32[]{:S(2)}) collective-permute-start(f32[584,128]{1,0:T(8,128)} %get-tuple-element.45.after), channel_id=1, source_target_pairs={{0,2},{1,3},{2,0},{3,1},{4,6},{5,7},{6,4},{7,5},{8,10},{9,11},{10,... | collective-permute-start | bytes 897032 | tf_op jit(solution)/shard_map/ppermute | solution.py:457
  10.5 2.5 %collective-permute-start.5 = (f32[584,128]{1,0:T(8,128)}, f32[584,128]{1,0:T(8,128)S(1)}, u32[]{:S(2)}, u32[]{:S(2)}) collective-permute-start(f32[584,128]{1,0:T(8,128)} %get-tuple-element.45.after), channel_id=1, source_target_pairs={{0,6},{1,7},{2,4},{3,5},{4,2},{5,3},{6,0},{7,1},{8,14},{9,15},{10,... | collective-permute-start | bytes 897032 | tf_op jit(solution)/shard_map/ppermute | solution.py:457
  13.0 0.1 collective-permute-start.4
  13.1 5.2 %collective-permute-done.refs_0_ = f32[584,128]{1,0:T(8,128)S(1)} collective-permute-done((f32[584,128]{1,0:T(8,128)}, f32[584,128]{1,0:T(8,128)S(1)}, u32[]{:S(2)}, u32[]{:S(2)}) %collective-permute-start) | collective-permute-done | bytes 299040 | tf_op jit(solution)/shard_map/ppermute | solution.py:457
  18.3 1.5 %collective-permute-start.1 = (f32[5,64,128]{2,1,0:T(8,128)}, f32[5,64,128]{2,1,0:T(8,128)S(1)}, u32[]{:S(2)}, u32[]{:S(2)}) collective-permute-start(f32[5,64,128]{2,1,0:T(8,128)} %get-tuple-element.47), channel_id=1, source_target_pairs={{0,8},{8,0},{16,24},{24,16},{1,9},{9,1},{17,25},{25,17},{2,10},{10... | collective-permute-start | bytes 491528 | tf_op jit(solution)/shard_map/ppermute | solution.py:481
  19.8 1.5 %collective-permute-start.2 = (f32[5,64,128]{2,1,0:T(8,128)}, f32[5,64,128]{2,1,0:T(8,128)S(1)}, u32[]{:S(2)}, u32[]{:S(2)}) collective-permute-start(f32[5,64,128]{2,1,0:T(8,128)} %get-tuple-element.48), channel_id=1, source_target_pairs={{0,16},{8,24},{16,0},{24,8},{1,17},{9,25},{17,1},{25,9},{2,18},{10... | collective-permute-start | bytes 491528 | tf_op jit(solution)/shard_map/ppermute | solution.py:481
  21.3 0.5 collective-permute-start.3
  21.8 2.7 %spread.1 = f32[64,64,128]{2,1,0:T(8,128)} custom-call(s32[64]{0:T(128)} %send.1, f32[32,64,128]{2,1,0:T(8,128)} %get-tuple-element.40.coef), custom_call_target="tpu_custom_call" | custom-call | bytes 4000000 | tf_op jit(solution)/shard_map/spread/pallas_call | solution.py:158
  24.5 3.1 %collective-permute-done.5.refs_2_ = f32[584,128]{1,0:T(8,128)S(1)} collective-permute-done((f32[584,128]{1,0:T(8,128)}, f32[584,128]{1,0:T(8,128)S(1)}, u32[]{:S(2)}, u32[]{:S(2)}) %collective-permute-start.5) | collective-permute-done | bytes 299040 | tf_op jit(solution)/shard_map/ppermute | solution.py:457
  27.7 11.7 %collective-permute-done.4.refs_1_ = f32[584,128]{1,0:T(8,128)S(1)} collective-permute-done((f32[584,128]{1,0:T(8,128)}, f32[584,128]{1,0:T(8,128)S(1)}, u32[]{:S(2)}, u32[]{:S(2)}) %collective-permute-start.4) | collective-permute-done | bytes 299040 | tf_op jit(solution)/shard_map/ppermute | solution.py:457
  39.4 0.0 collective-permute-done.1.refs_1_
  39.4 0.0 collective-permute-done.2.refs_2_
  39.4 0.0 collective-permute-done.3.refs_3_
  39.4 4.9 %all-to-all-start = ((f32[64,64,128]{2,1,0:T(8,128)}), f32[64,64,128]{2,1,0:T(8,128)S(1)}, u32[]{:S(2)}, u32[]{:S(2)}) async-start(f32[64,64,128]{2,1,0:T(8,128)} %spread.1), calls=%async_computation | async-start | bytes 4194304 | tf_op jit(solution)/shard_map/all_to_all | solution.py:488
  44.3 0.0 copy-done.5
  44.3 2.7 %select.31 = (f32[15,64,128]{2,1,0:T(8,128)}, f32[15,64,128]{2,1,0:T(8,128)}, f32[15,64,128]{2,1,0:T(8,128)}, f32[15,64,128]{2,1,0:T(8,128)}) custom-call(s32[1]{0:T(128)} %bitcast.group_at, s32[1]{0:T(128)} %bitcast.1.lane_at.position, f32[584,128]{1,0:T(8,128)} %copy-done.5, f32[584,128]{1,0:T(8,128)} %copy-done.7, f32[584,128]{1,0:T(8,128)} %copy-done.6), custom_call_target="tpu_custom_call" | custom-call | bytes 4000000 | tf_op jit(solution)/shard_map/select/pallas_call | solution.py:208
  47.0 1.8 %collective-permute-start.6 = (f32[15,64,128]{2,1,0:T(8,128)}, f32[15,64,128]{2,1,0:T(8,128)S(1)}, u32[]{:S(2)}, u32[]{:S(2)}) collective-permute-start(f32[15,64,128]{2,1,0:T(8,128)} %get-tuple-element.54), channel_id=1, source_target_pairs={{0,8},{8,0},{16,24},{24,16},{1,9},{9,1},{17,25},{25,17},{2,10},{10... | collective-permute-start | bytes 1474568 | tf_op jit(solution)/shard_map/ppermute | solution.py:481
  48.9 1.5 %collective-permute-start.11 = (f32[15,64,128]{2,1,0:T(8,128)}, f32[15,64,128]{2,1,0:T(8,128)}, u32[]{:S(2)}, u32[]{:S(2)}) collective-permute-start(f32[15,64,128]{2,1,0:T(8,128)} %get-tuple-element.65), channel_id=1, source_target_pairs={{0,16},{8,24},{16,0},{24,8},{1,17},{9,25},{17,1},{25,9},{2,18},{10... | collective-permute-start | bytes 1474568 | tf_op jit(solution)/shard_map/ppermute | solution.py:481
  50.3 0.3 collective-permute-start.12
  50.6 0.2 dynamic-slice_reduce_fusion
  50.8 0.0 copy-start.17
  50.8 0.0 copy-start.16
  50.8 0.0 copy-start.1
  50.8 0.0 copy-start.2
  50.8 12.3 %prepare.1 = (bf16[32,128,832]{2,1,0:T(8,128)(2,1)}, bf16[32,256,128]{2,1,0:T(8,128)(2,1)}, bf16[8,128,2112]{2,1,0:T(8,128)(2,1)}) custom-call(f32[584,128]{1,0:T(8,128)} %get-tuple-element.45.after, f32[32,64,768]{2,1,0:T(8,128)} %coupling.1, f32[32,64,256]{2,1,0:T(8,128)} %basis.3, f32[32,64,64]{2,1,0:T(8,128)} %transfer.3, f32[8,64,2048]{2,1,0:T(8,128)} %mid_coupling.1, ...), custom_call_target="tpu_custom_call" | custom-call | bytes 30000000 | tf_op jit(solution)/shard_map/prepare/pallas_call | solution.py:245
  63.2 0.0 collective-permute-start.7
  63.2 0.5 collective-permute-start.8
  63.7 0.8 collective-permute-done.7.refs_8_
  64.6 0.1 collective-permute-start.9
  64.7 0.1 collective-permute-done.8.refs_9_
  64.8 0.3 collective-permute-start.10
  65.1 0.9 collective-permute-done.9.refs_10_
  66.0 0.1 collective-permute-start.13
  66.1 0.3 collective-permute-done.10.refs_11_
  66.4 8.4 %collective-permute-done.6.refs_5_ = f32[15,64,128]{2,1,0:T(8,128)S(1)} collective-permute-done((f32[15,64,128]{2,1,0:T(8,128)}, f32[15,64,128]{2,1,0:T(8,128)S(1)}, u32[]{:S(2)}, u32[]{:S(2)}) %collective-permute-start.6) | collective-permute-done | bytes 491552 | tf_op jit(solution)/shard_map/ppermute | solution.py:481
  74.8 3.1 %collective-permute-done.11.refs_6_ = f32[15,64,128]{2,1,0:T(8,128)} collective-permute-done((f32[15,64,128]{2,1,0:T(8,128)}, f32[15,64,128]{2,1,0:T(8,128)}, u32[]{:S(2)}, u32[]{:S(2)}) %collective-permute-start.11) | collective-permute-done | bytes 491552 | tf_op jit(solution)/shard_map/ppermute | solution.py:481
  77.9 0.0 collective-permute-start.15
  77.9 12.2 %collective-permute-done.12.refs_7_ = f32[15,64,128]{2,1,0:T(8,128)} collective-permute-done((f32[15,64,128]{2,1,0:T(8,128)}, f32[15,64,128]{2,1,0:T(8,128)}, u32[]{:S(2)}, u32[]{:S(2)}) %collective-permute-start.12) | collective-permute-done | bytes 491552 | tf_op jit(solution)/shard_map/ppermute | solution.py:481
  90.1 0.0 collective-permute-start.16
  90.1 0.5 collective-permute-start.14
  90.6 0.1 copy.15.pair_leaf
  90.7 0.0 collective-permute-done.13.refs_12_
  90.7 0.0 collective-permute-done.15.refs_14_
  90.7 1.6 %collective-permute-done.16.refs_15_ = f32[15,64,128]{2,1,0:T(8,128)} collective-permute-done((f32[15,64,128]{2,1,0:T(8,128)}, f32[15,64,128]{2,1,0:T(8,128)}, u32[]{:S(2)}, u32[]{:S(2)}) %collective-permute-start.16) | collective-permute-done | bytes 491552 | tf_op jit(solution)/shard_map/ppermute | solution.py:494
  92.3 0.5 collective-permute-done.14.refs_13_
  92.8 1.6 %all-to-all-done.refs_16_ = f32[64,64,128]{2,1,0:T(8,128)S(1)} async-done(((f32[64,64,128]{2,1,0:T(8,128)}), f32[64,64,128]{2,1,0:T(8,128)S(1)}, u32[]{:S(2)}, u32[]{:S(2)}) %all-to-all-start) | async-done | bytes 2097184 | tf_op jit(solution)/shard_map/all_to_all | solution.py:488
  94.4 13.0 %tail.1 = f32[8192,128]{1,0:T(8,128)} custom-call(s32[32]{0:T(128)S(1)} %copy-done.1, s32[8,32]{1,0:T(8,128)S(1)} %fusion.7.pair, s32[1]{0:T(128)} %bitcast.1.lane_at.position, s32[4]{0:T(128)S(1)} %and_select_fusion.3.tops, s32[32]{0:T(128)S(1)} %copy-done.2, s32[32,12]{1,0:T(8,128)S(1)} %copy.15.pair_leaf, f32[5,64,128]{2,1,0:T(8,128)} %get-tuple-element.55.refs_0_, ...), custom_call_target="tpu_custom_call" | custom-call | flops 6000000000 | bytes 20000000 | tf_op jit(solution)/shard_map/tail/pallas_call | solution.py:419
  (33 shorter events, 0.1 us)
Async XLA Ops:
  0.0 50.6 %copy-start = (s32[8,4]{0,1:T(4,128)S(1)}, s32[8,4]{0,1:T(4,128)}, u32[]{:S(2)}) copy-start(s32[8,4]{0,1:T(4,128)} %param.26) | copy-start | bytes 388
  7.4 10.9 %collective-permute-start = (f32[584,128]{1,0:T(8,128)}, f32[584,128]{1,0:T(8,128)S(1)}, u32[]{:S(2)}, u32[]{:S(2)}) collective-permute-start(f32[584,128]{1,0:T(8,128)} %get-tuple-element.45.after), channel_id=1, source_target_pairs={{0,2},{1,3},{2,0},{3,1},{4,6},{5,7},{6,4},{7,5},{8,10},{9,11},{10,... | collective-permute-start | bytes 897032 | tf_op jit(solution)/shard_map/ppermute | solution.py:457
  10.5 17.2 %collective-permute-start.5 = (f32[584,128]{1,0:T(8,128)}, f32[584,128]{1,0:T(8,128)S(1)}, u32[]{:S(2)}, u32[]{:S(2)}) collective-permute-start(f32[584,128]{1,0:T(8,128)} %get-tuple-element.45.after), channel_id=1, source_target_pairs={{0,6},{1,7},{2,4},{3,5},{4,2},{5,3},{6,0},{7,1},{8,14},{9,15},{10,... | collective-permute-start | bytes 897032 | tf_op jit(solution)/shard_map/ppermute | solution.py:457
  13.0 26.4 %collective-permute-start.4 = (f32[584,128]{1,0:T(8,128)}, f32[584,128]{1,0:T(8,128)S(1)}, u32[]{:S(2)}, u32[]{:S(2)}) collective-permute-start(f32[584,128]{1,0:T(8,128)} %get-tuple-element.45.after), channel_id=1, source_target_pairs={{0,4},{1,5},{2,6},{3,7},{4,0},{5,1},{6,2},{7,3},{8,12},{9,13},{10,... | collective-permute-start | bytes 897032 | tf_op jit(solution)/shard_map/ppermute | solution.py:457
  18.3 26.0 %copy-start.5 = (f32[584,128]{1,0:T(8,128)}, f32[584,128]{1,0:T(8,128)S(1)}, u32[]{:S(2)}) copy-start(f32[584,128]{1,0:T(8,128)S(1)} %collective-permute-done.refs_0_) | copy-start | bytes 897028
  18.3 21.1 %collective-permute-start.1 = (f32[5,64,128]{2,1,0:T(8,128)}, f32[5,64,128]{2,1,0:T(8,128)S(1)}, u32[]{:S(2)}, u32[]{:S(2)}) collective-permute-start(f32[5,64,128]{2,1,0:T(8,128)} %get-tuple-element.47), channel_id=1, source_target_pairs={{0,8},{8,0},{16,24},{24,16},{1,9},{9,1},{17,25},{25,17},{2,10},{10... | collective-permute-start | bytes 491528 | tf_op jit(solution)/shard_map/ppermute | solution.py:481
  19.8 19.6 %collective-permute-start.2 = (f32[5,64,128]{2,1,0:T(8,128)}, f32[5,64,128]{2,1,0:T(8,128)S(1)}, u32[]{:S(2)}, u32[]{:S(2)}) collective-permute-start(f32[5,64,128]{2,1,0:T(8,128)} %get-tuple-element.48), channel_id=1, source_target_pairs={{0,16},{8,24},{16,0},{24,8},{1,17},{9,25},{17,1},{25,9},{2,18},{10... | collective-permute-start | bytes 491528 | tf_op jit(solution)/shard_map/ppermute | solution.py:481
  21.3 18.1 %collective-permute-start.3 = (f32[5,64,128]{2,1,0:T(8,128)}, f32[5,64,128]{2,1,0:T(8,128)}, u32[]{:S(2)}, u32[]{:S(2)}) collective-permute-start(f32[5,64,128]{2,1,0:T(8,128)} %get-tuple-element.49), channel_id=1, source_target_pairs={{0,24},{8,16},{16,8},{24,0},{1,25},{9,17},{17,9},{25,1},{2,26},{10... | collective-permute-start | bytes 491528 | tf_op jit(solution)/shard_map/ppermute | solution.py:481
  27.7 16.6 %copy-start.6 = (f32[584,128]{1,0:T(8,128)}, f32[584,128]{1,0:T(8,128)S(1)}, u32[]{:S(2)}) copy-start(f32[584,128]{1,0:T(8,128)S(1)} %collective-permute-done.5.refs_2_) | copy-start | bytes 897028
  39.4 4.9 %copy-start.7 = (f32[584,128]{1,0:T(8,128)}, f32[584,128]{1,0:T(8,128)S(1)}, u32[]{:S(2)}) copy-start(f32[584,128]{1,0:T(8,128)S(1)} %collective-permute-done.4.refs_1_) | copy-start | bytes 897028
  39.4 23.8 %copy-start.9 = (f32[5,64,128]{2,1,0:T(8,128)}, f32[5,64,128]{2,1,0:T(8,128)S(1)}, u32[]{:S(2)}) copy-start(f32[5,64,128]{2,1,0:T(8,128)S(1)} %collective-permute-done.1.refs_1_) | copy-start | bytes 491524
  39.4 7.6 %copy-start.10 = (f32[5,64,128]{2,1,0:T(8,128)}, f32[5,64,128]{2,1,0:T(8,128)S(1)}, u32[]{:S(2)}) copy-start(f32[5,64,128]{2,1,0:T(8,128)S(1)} %collective-permute-done.2.refs_2_) | copy-start | bytes 491524
  39.4 55.0 %all-to-all-start = ((f32[64,64,128]{2,1,0:T(8,128)}), f32[64,64,128]{2,1,0:T(8,128)S(1)}, u32[]{:S(2)}, u32[]{:S(2)}) async-start(f32[64,64,128]{2,1,0:T(8,128)} %spread.1), calls=%async_computation | async-start | bytes 4194304 | tf_op jit(solution)/shard_map/all_to_all | solution.py:488
  47.0 27.8 %collective-permute-start.6 = (f32[15,64,128]{2,1,0:T(8,128)}, f32[15,64,128]{2,1,0:T(8,128)S(1)}, u32[]{:S(2)}, u32[]{:S(2)}) collective-permute-start(f32[15,64,128]{2,1,0:T(8,128)} %get-tuple-element.54), channel_id=1, source_target_pairs={{0,8},{8,0},{16,24},{24,16},{1,9},{9,1},{17,25},{25,17},{2,10},{10... | collective-permute-start | bytes 1474568 | tf_op jit(solution)/shard_map/ppermute | solution.py:481
  48.9 29.0 %collective-permute-start.11 = (f32[15,64,128]{2,1,0:T(8,128)}, f32[15,64,128]{2,1,0:T(8,128)}, u32[]{:S(2)}, u32[]{:S(2)}) collective-permute-start(f32[15,64,128]{2,1,0:T(8,128)} %get-tuple-element.65), channel_id=1, source_target_pairs={{0,16},{8,24},{16,0},{24,8},{1,17},{9,25},{17,1},{25,9},{2,18},{10... | collective-permute-start | bytes 1474568 | tf_op jit(solution)/shard_map/ppermute | solution.py:481
  50.3 39.7 %collective-permute-start.12 = (f32[15,64,128]{2,1,0:T(8,128)}, f32[15,64,128]{2,1,0:T(8,128)}, u32[]{:S(2)}, u32[]{:S(2)}) collective-permute-start(f32[15,64,128]{2,1,0:T(8,128)} %get-tuple-element.66), channel_id=1, source_target_pairs={{0,24},{8,16},{16,8},{24,0},{1,25},{9,17},{17,9},{25,1},{2,26},{10... | collective-permute-start | bytes 1474568 | tf_op jit(solution)/shard_map/ppermute | solution.py:481
  50.8 12.4 %copy-start.8 = (f32[5,64,128]{2,1,0:T(8,128)S(1)}, f32[5,64,128]{2,1,0:T(8,128)}, u32[]{:S(2)}) copy-start(f32[5,64,128]{2,1,0:T(8,128)} %get-tuple-element.55.refs_0_) | copy-start | bytes 491524
  50.8 12.9 %copy-start.17 = (s32[8,32]{1,0:T(8,128)S(1)}, s32[8,32]{1,0:T(8,128)}, u32[]{:S(2)}) copy-start(s32[8,32]{1,0:T(8,128)} %param.24) | copy-start | bytes 3076
  50.8 13.8 %copy-start.11 = (f32[5,64,128]{2,1,0:T(8,128)S(1)}, f32[5,64,128]{2,1,0:T(8,128)}, u32[]{:S(2)}) copy-start(f32[5,64,128]{2,1,0:T(8,128)} %copy-done.10) | copy-start | bytes 491524
  50.8 15.2 %copy-start.3 = (f32[15,64,128]{2,1,0:T(8,128)S(1)}, f32[15,64,128]{2,1,0:T(8,128)}, u32[]{:S(2)}) copy-start(f32[15,64,128]{2,1,0:T(8,128)} %get-tuple-element.63.refs_4_) | copy-start | bytes 1474564
  50.8 39.8 %copy-start.16 = (s32[32,12]{0,1:T(8,128)S(1)}, s32[32,12]{0,1:T(8,128)}, u32[]{:S(2)}) copy-start(s32[32,12]{0,1:T(8,128)} %param.21) | copy-start | bytes 4612
  50.8 43.6 %copy-start.1 = (s32[32]{0:T(128)S(1)}, s32[32]{0:T(128)}, u32[]{:S(2)}) copy-start(s32[32]{0:T(128)} %parent.3) | copy-start | bytes 388
  50.8 43.6 %copy-start.2 = (s32[32]{0:T(128)S(1)}, s32[32]{0:T(128)}, u32[]{:S(2)}) copy-start(s32[32]{0:T(128)} %size.3) | copy-start | bytes 388
  63.2 1.4 %collective-permute-start.7 = (f32[5,64,128]{2,1,0:T(8,128)S(1)}, f32[5,64,128]{2,1,0:T(8,128)S(1)}, u32[]{:S(2)}, u32[]{:S(2)}) collective-permute-start(f32[5,64,128]{2,1,0:T(8,128)S(1)} %copy-done.8), channel_id=1, source_target_pairs={{0,1},{1,0},{2,3},{3,2},{4,5},{5,4},{6,7},{7,6},{8,9},{9,8},{10,11... | collective-permute-start | bytes 491528 | tf_op jit(solution)/shard_map/ppermute | solution.py:489
  63.2 1.6 %collective-permute-start.8 = (f32[5,64,128]{2,1,0:T(8,128)S(1)}, f32[5,64,128]{2,1,0:T(8,128)S(1)}, u32[]{:S(2)}, u32[]{:S(2)}) collective-permute-start(f32[5,64,128]{2,1,0:T(8,128)S(1)} %collective-permute-done.1.refs_1_), channel_id=1, source_target_pairs={{0,1},{1,0},{2,3},{3,2},{4,5},{5,4},{6,7},{7,6},{8,9},{9,8},{10,11... | collective-permute-start | bytes 491528 | tf_op jit(solution)/shard_map/ppermute | solution.py:489
  64.6 25.5 %copy-start.12 = (f32[5,64,128]{2,1,0:T(8,128)}, f32[5,64,128]{2,1,0:T(8,128)S(1)}, u32[]{:S(2)}) copy-start(f32[5,64,128]{2,1,0:T(8,128)S(1)} %collective-permute-done.7.refs_8_) | copy-start | bytes 491524
  64.6 1.4 %collective-permute-start.9 = (f32[5,64,128]{2,1,0:T(8,128)S(1)}, f32[5,64,128]{2,1,0:T(8,128)S(1)}, u32[]{:S(2)}, u32[]{:S(2)}) collective-permute-start(f32[5,64,128]{2,1,0:T(8,128)S(1)} %copy-done.11), channel_id=1, source_target_pairs={{0,1},{1,0},{2,3},{3,2},{4,5},{5,4},{6,7},{7,6},{8,9},{9,8},{10,11... | collective-permute-start | bytes 491528 | tf_op jit(solution)/shard_map/ppermute | solution.py:489
  64.8 25.3 %copy-start.13 = (f32[5,64,128]{2,1,0:T(8,128)}, f32[5,64,128]{2,1,0:T(8,128)S(1)}, u32[]{:S(2)}) copy-start(f32[5,64,128]{2,1,0:T(8,128)S(1)} %collective-permute-done.8.refs_9_) | copy-start | bytes 491524
  64.8 1.6 %collective-permute-start.10 = (f32[5,64,128]{2,1,0:T(8,128)}, f32[5,64,128]{2,1,0:T(8,128)S(1)}, u32[]{:S(2)}, u32[]{:S(2)}) collective-permute-start(f32[5,64,128]{2,1,0:T(8,128)} %collective-permute-done.3.refs_3_), channel_id=1, source_target_pairs={{0,1},{1,0},{2,3},{3,2},{4,5},{5,4},{6,7},{7,6},{8,9},{9,8},{10,11... | collective-permute-start | bytes 491528 | tf_op jit(solution)/shard_map/ppermute | solution.py:489
  66.0 28.4 %copy-start.14 = (f32[5,64,128]{2,1,0:T(8,128)}, f32[5,64,128]{2,1,0:T(8,128)S(1)}, u32[]{:S(2)}) copy-start(f32[5,64,128]{2,1,0:T(8,128)S(1)} %collective-permute-done.9.refs_10_) | copy-start | bytes 491524
  66.0 24.7 %collective-permute-start.13 = (f32[15,64,128]{2,1,0:T(8,128)S(1)}, f32[15,64,128]{2,1,0:T(8,128)}, u32[]{:S(2)}, u32[]{:S(2)}) collective-permute-start(f32[15,64,128]{2,1,0:T(8,128)S(1)} %copy-done.3), channel_id=1, source_target_pairs={{0,1},{1,0},{2,3},{3,2},{4,5},{5,4},{6,7},{7,6},{8,9},{9,8},{10,11... | collective-permute-start | bytes 1474568 | tf_op jit(solution)/shard_map/ppermute | solution.py:494
  66.4 28.0 %copy-start.15 = (f32[5,64,128]{2,1,0:T(8,128)}, f32[5,64,128]{2,1,0:T(8,128)S(1)}, u32[]{:S(2)}) copy-start(f32[5,64,128]{2,1,0:T(8,128)S(1)} %collective-permute-done.10.refs_11_) | copy-start | bytes 491524
  74.8 19.6 %copy-start.4 = (f32[15,64,128]{2,1,0:T(8,128)}, f32[15,64,128]{2,1,0:T(8,128)S(1)}, u32[]{:S(2)}) copy-start(f32[15,64,128]{2,1,0:T(8,128)S(1)} %collective-permute-done.6.refs_5_) | copy-start | bytes 1474564
  77.9 12.8 %collective-permute-start.15 = (f32[15,64,128]{2,1,0:T(8,128)}, f32[15,64,128]{2,1,0:T(8,128)}, u32[]{:S(2)}, u32[]{:S(2)}) collective-permute-start(f32[15,64,128]{2,1,0:T(8,128)} %collective-permute-done.11.refs_6_), channel_id=1, source_target_pairs={{0,1},{1,0},{2,3},{3,2},{4,5},{5,4},{6,7},{7,6},{8,9},{9,8},{10,11... | collective-permute-start | bytes 1474568 | tf_op jit(solution)/shard_map/ppermute | solution.py:494
  90.1 2.2 %collective-permute-start.16 = (f32[15,64,128]{2,1,0:T(8,128)}, f32[15,64,128]{2,1,0:T(8,128)}, u32[]{:S(2)}, u32[]{:S(2)}) collective-permute-start(f32[15,64,128]{2,1,0:T(8,128)} %collective-permute-done.12.refs_7_), channel_id=1, source_target_pairs={{0,1},{1,0},{2,3},{3,2},{4,5},{5,4},{6,7},{7,6},{8,9},{9,8},{10,11... | collective-permute-start | bytes 1474568 | tf_op jit(solution)/shard_map/ppermute | solution.py:494
  90.1 2.7 %collective-permute-start.14 = (f32[15,64,128]{2,1,0:T(8,128)S(1)}, f32[15,64,128]{2,1,0:T(8,128)}, u32[]{:S(2)}, u32[]{:S(2)}) collective-permute-start(f32[15,64,128]{2,1,0:T(8,128)S(1)} %collective-permute-done.6.refs_5_), channel_id=1, source_target_pairs={{0,1},{1,0},{2,3},{3,2},{4,5},{5,4},{6,7},{7,6},{8,9},{9,8},{10,11... | collective-permute-start | bytes 1474568 | tf_op jit(solution)/shard_map/ppermute | solution.py:494

commit v2 on v1

--- a/solution.py
+++ b/solution.py
@@ -269,7 +269,7 @@
     scratch = refs[2 * count + 6 :]
     held_messages, scratch = scratch[: 2 * count], scratch[2 * count :]
     (
-        arrived_held, mid_wide_held, top_held, wide_held, basis_held, parts, top_parts, leaf_parts, out_held,
+        arrived_held, mid_wide_held, top_held, wide_held, basis_held, parts, top_parts, leaf_parts, near_top, out_held,
         message_sem, arrived_sem, mid_sem, top_sem, wide_sem, basis_sem, out_sem,
     ) = scratch
     mids, leaves, points = mid_wide.shape[0], wide.shape[0], basis.shape[1]
@@ -342,18 +342,14 @@
             copy.start()
     fetch_top.wait()
     stacked = jnp.concatenate([top_parts[tops[k]] for k in range(tops.shape[0])], axis=0)
-    parts[slots + 1] = lanes_of(fold(dot(rows_of(top_held[...]), stacked)))
+    near_top[...] = lanes_of(fold(dot(rows_of(top_held[...]), stacked)))
     for c in range(mids):
         fetch_mid(c).wait()
 
-    @pl.loop(0, mids, step=4)
-    def _(start):
-        values = []
-        for g in range(4):
-            blocks = [parts[pair[start + g, k]] for k in range(pair.shape[1])] + [parts[slots + 1]]
-            values.append(fold(dot(mid_wide_held[start + g], jnp.concatenate(blocks, axis=0))))
-        for g in range(4):
-            leaf_parts[slots + 1 + start + g] = lanes_of(values[g])
+    for c in range(mids):
+        blocks = [parts[pair[c, k]] for k in range(pair.shape[1])] + [near_top[...]]
+        value = fold(dot(mid_wide_held[c], jnp.concatenate(blocks, axis=0)))
+        leaf_parts[slots + 1 + c] = lanes_of(value)
 
     point = lax.broadcasted_iota(jnp.int32, (points, ports), 0)
 
@@ -362,25 +358,30 @@
         target = out.at[pl.ds(index * rows, rows), :]
         return pltpu.make_async_copy(out_held.at[index % 2], target, out_sem.at[index % 2])
 
-    for index in range(steps):
-        if index + ahead < steps:
-            for copy in fetch_leaves(index + ahead):
-                copy.start()
-        for copy in fetch_leaves(index):
-            copy.wait()
+    before = None
+    for index in range(steps + 1):
         values = []
-        for g in range(group):
-            leaf = index * group + g
-            blocks = [leaf_parts[pair_leaf[leaf, k]] for k in range(pair_leaf.shape[1])]
-            blocks.append(leaf_parts[slots + 1 + parent[leaf]])
-            values.append(fold(dot(wide_held[leaf], jnp.concatenate(blocks, axis=0))))
-        if index >= 2:
-            send(index - 2).wait()
-        for g in range(group):
-            far = deep_dot(basis_held[index * group + g], values[g])
-            far = jnp.where(point < size[index * group + g], far, 0.0)
-            out_held[index % 2, g * points : (g + 1) * points, :] = far
-        send(index).start()
+        if index < steps:
+            if index + ahead < steps:
+                for copy in fetch_leaves(index + ahead):
+                    copy.start()
+            for copy in fetch_leaves(index):
+                copy.wait()
+        if index >= 3:
+            send(index - 3).wait()
+        if index < steps:
+            for g in range(group):
+                leaf = index * group + g
+                blocks = [leaf_parts[pair_leaf[leaf, k]] for k in range(pair_leaf.shape[1])]
+                blocks.append(leaf_parts[slots + 1 + parent[leaf]])
+                values.append(fold(dot(wide_held[leaf], jnp.concatenate(blocks, axis=0))))
+        if before is not None:
+            for g in range(group):
+                leaf = (index - 1) * group + g
+                far = jnp.where(point < size[leaf], deep_dot(basis_held[leaf], before[g]), 0.0)
+                out_held[(index - 1) % 2, g * points : (g + 1) * points, :] = far
+            send(index - 1).start()
+        before = values
     for index in range(max(0, steps - 2), steps):
         send(index).wait()
 
@@ -405,9 +406,10 @@
         (top_coupling.shape[1:], full),
         (wide.shape, half),
         (basis.shape, half),
-        ((slots + 2, rank, 2 * ports), half),
+        ((slots + 1, rank, 2 * ports), half),
         ((owners + 1, rank, 2 * ports), half),
         ((slots + 1 + mids, rank, 2 * ports), half),
+        ((rank, 2 * ports), half),
         ((2, group * points, ports), full),
     ]
     semaphores = [(2 * len(near_side),), (2,), (mids,), (), (leaves // group,), (leaves // group,), (2,)]

time: 108 us -> 108 us (level)
  no operation moved by 1% of the time
where the time goes in v2:
time: 108 us; the launch traced here: 107 us
  waiting for transfers between devices  49.5 us (46%)
  Pallas kernels  37.9 us (35%)
  starting transfers between devices  19.2 us (18%)
    ppermute x6, waiting for transfers between devices, body(): lax.ppermute(messages[d], 'group', [(g, g ^ d) for g in range(groups)])  23.6 us
    ppermute x3, waiting for transfers between devices, body(): lax.ppermute(lifted, 'cluster', [(c, c ^ 2 * d) for c in range(per_cluste...  20 us
    pallas_call x1, Pallas kernels, tail(): pl.pallas_call(functools.partial(tail_kernel, (bounds, per_pair, groups,...  12.7 us
    pallas_call x1, Pallas kernels, prepare(): pl.pallas_call(prepare_kernel, grid=(steps,), in_specs=[pl.BlockSpec(memo...  12.3 us
    pallas_call x1, Pallas kernels, up_sweep(): pl.pallas_call(functools.partial(up_kernel, sizes), grid_spec=pltpu.Prefe...  7.43 us
    ppermute x6, starting transfers between devices, body(): lax.ppermute(messages[d], 'group', [(g, g ^ d) for g in range(groups)])  7.04 us
    ppermute x3, starting transfers between devices, body(): lax.ppermute(lifted, 'cluster', [(c, c ^ 2 * d) for c in range(per_cluste...  5.65 us
    all_to_all x1, starting transfers between devices, body(): lax.all_to_all(outgoing, AXES, split_axis=0, concat_axis=0, tiled=True)  4.86 us
  transfers between devices with their start and end apart: 18, of which 13 were waited for; matrix products, arithmetic and copies ran while one was open for 0% of the time, Pallas kernels for 17%

profile of v2, /device:TPU:0, one launch (start us, length us, event | category | flops | bytes accessed | tf_op | source)
XLA Modules:
  0.0 107.1 jit_solution(13377119884399199364)
XLA Ops:
  0.0 7.4 %up_sweep.1 = (f32[32,64,128]{2,1,0:T(8,128)}, f32[584,128]{1,0:T(8,128)}, f32[5,64,128]{2,1,0:T(8,128)}, f32[5,64,128]{2,1,0:T(8,128)}, f32[5,64,128]{2,1,0:T(8,128)}, /*index=5*/f32[5,64,128]{2,1,0:T(8,128)}) custom-call(s32[32]{0:T(128)} %size.3, s32[32]{0:T(128)} %parent.3, s32[64]{0:T(128)} %slots.1, s32[1]{0:T(128)} %bitcast.group_at, ...), custom_call_target="tpu_custom_call" | custom-call | flops 1000000000 | bytes 10000000 | tf_op jit(solution)/shard_map/up_sweep/pallas_call | solution.py:120
  7.4 3.1 %collective-permute-start = (f32[584,128]{1,0:T(8,128)}, f32[584,128]{1,0:T(8,128)S(1)}, u32[]{:S(2)}, u32[]{:S(2)}) collective-permute-start(f32[584,128]{1,0:T(8,128)} %get-tuple-element.45.after), channel_id=1, source_target_pairs={{0,2},{1,3},{2,0},{3,1},{4,6},{5,7},{6,4},{7,5},{8,10},{9,11},{10,... | collective-permute-start | bytes 897032 | tf_op jit(solution)/shard_map/ppermute | solution.py:459
  10.5 2.5 %collective-permute-start.5 = (f32[584,128]{1,0:T(8,128)}, f32[584,128]{1,0:T(8,128)S(1)}, u32[]{:S(2)}, u32[]{:S(2)}) collective-permute-start(f32[584,128]{1,0:T(8,128)} %get-tuple-element.45.after), channel_id=1, source_target_pairs={{0,6},{1,7},{2,4},{3,5},{4,2},{5,3},{6,0},{7,1},{8,14},{9,15},{10,... | collective-permute-start | bytes 897032 | tf_op jit(solution)/shard_map/ppermute | solution.py:459
  13.0 0.1 collective-permute-start.4
  13.1 5.2 %collective-permute-done.refs_0_ = f32[584,128]{1,0:T(8,128)S(1)} collective-permute-done((f32[584,128]{1,0:T(8,128)}, f32[584,128]{1,0:T(8,128)S(1)}, u32[]{:S(2)}, u32[]{:S(2)}) %collective-permute-start) | collective-permute-done | bytes 299040 | tf_op jit(solution)/shard_map/ppermute | solution.py:459
  18.3 1.5 %collective-permute-start.1 = (f32[5,64,128]{2,1,0:T(8,128)}, f32[5,64,128]{2,1,0:T(8,128)S(1)}, u32[]{:S(2)}, u32[]{:S(2)}) collective-permute-start(f32[5,64,128]{2,1,0:T(8,128)} %get-tuple-element.47), channel_id=1, source_target_pairs={{0,8},{8,0},{16,24},{24,16},{1,9},{9,1},{17,25},{25,17},{2,10},{10... | collective-permute-start | bytes 491528 | tf_op jit(solution)/shard_map/ppermute | solution.py:483
  19.8 1.5 %collective-permute-start.2 = (f32[5,64,128]{2,1,0:T(8,128)}, f32[5,64,128]{2,1,0:T(8,128)S(1)}, u32[]{:S(2)}, u32[]{:S(2)}) collective-permute-start(f32[5,64,128]{2,1,0:T(8,128)} %get-tuple-element.48), channel_id=1, source_target_pairs={{0,16},{8,24},{16,0},{24,8},{1,17},{9,25},{17,1},{25,9},{2,18},{10... | collective-permute-start | bytes 491528 | tf_op jit(solution)/shard_map/ppermute | solution.py:483
  21.3 0.5 collective-permute-start.3
  21.8 2.7 %spread.1 = f32[64,64,128]{2,1,0:T(8,128)} custom-call(s32[64]{0:T(128)} %send.1, f32[32,64,128]{2,1,0:T(8,128)} %get-tuple-element.40.coef), custom_call_target="tpu_custom_call" | custom-call | bytes 4000000 | tf_op jit(solution)/shard_map/spread/pallas_call | solution.py:158
  24.5 3.1 %collective-permute-done.5.refs_2_ = f32[584,128]{1,0:T(8,128)S(1)} collective-permute-done((f32[584,128]{1,0:T(8,128)}, f32[584,128]{1,0:T(8,128)S(1)}, u32[]{:S(2)}, u32[]{:S(2)}) %collective-permute-start.5) | collective-permute-done | bytes 299040 | tf_op jit(solution)/shard_map/ppermute | solution.py:459
  27.6 11.7 %collective-permute-done.4.refs_1_ = f32[584,128]{1,0:T(8,128)S(1)} collective-permute-done((f32[584,128]{1,0:T(8,128)}, f32[584,128]{1,0:T(8,128)S(1)}, u32[]{:S(2)}, u32[]{:S(2)}) %collective-permute-start.4) | collective-permute-done | bytes 299040 | tf_op jit(solution)/shard_map/ppermute | solution.py:459
  39.4 0.0 collective-permute-done.1.refs_1_
  39.4 0.0 collective-permute-done.2.refs_2_
  39.4 0.0 collective-permute-done.3.refs_3_
  39.4 4.9 %all-to-all-start = ((f32[64,64,128]{2,1,0:T(8,128)}), f32[64,64,128]{2,1,0:T(8,128)S(1)}, u32[]{:S(2)}, u32[]{:S(2)}) async-start(f32[64,64,128]{2,1,0:T(8,128)} %spread.1), calls=%async_computation | async-start | bytes 4194304 | tf_op jit(solution)/shard_map/all_to_all | solution.py:490
  44.3 2.7 %select.31 = (f32[15,64,128]{2,1,0:T(8,128)}, f32[15,64,128]{2,1,0:T(8,128)}, f32[15,64,128]{2,1,0:T(8,128)}, f32[15,64,128]{2,1,0:T(8,128)}) custom-call(s32[1]{0:T(128)} %bitcast.group_at, s32[1]{0:T(128)} %bitcast.1.lane_at.position, f32[584,128]{1,0:T(8,128)} %copy-done.5, f32[584,128]{1,0:T(8,128)} %copy-done.7, f32[584,128]{1,0:T(8,128)} %copy-done.6), custom_call_target="tpu_custom_call" | custom-call | bytes 4000000 | tf_op jit(solution)/shard_map/select/pallas_call | solution.py:208
  47.0 1.8 %collective-permute-start.6 = (f32[15,64,128]{2,1,0:T(8,128)}, f32[15,64,128]{2,1,0:T(8,128)S(1)}, u32[]{:S(2)}, u32[]{:S(2)}) collective-permute-start(f32[15,64,128]{2,1,0:T(8,128)} %get-tuple-element.54), channel_id=1, source_target_pairs={{0,8},{8,0},{16,24},{24,16},{1,9},{9,1},{17,25},{25,17},{2,10},{10... | collective-permute-start | bytes 1474568 | tf_op jit(solution)/shard_map/ppermute | solution.py:483
  48.9 1.5 %collective-permute-start.11 = (f32[15,64,128]{2,1,0:T(8,128)}, f32[15,64,128]{2,1,0:T(8,128)}, u32[]{:S(2)}, u32[]{:S(2)}) collective-permute-start(f32[15,64,128]{2,1,0:T(8,128)} %get-tuple-element.65), channel_id=1, source_target_pairs={{0,16},{8,24},{16,0},{24,8},{1,17},{9,25},{17,1},{25,9},{2,18},{10... | collective-permute-start | bytes 1474568 | tf_op jit(solution)/shard_map/ppermute | solution.py:483
  50.3 0.3 collective-permute-start.12
  50.6 0.0 copy-done
  50.6 0.2 dynamic-slice_reduce_fusion
  50.8 0.0 copy-start.17
  50.8 0.0 copy-start.16
  50.8 0.0 copy-start.1
  50.8 0.0 copy-start.2
  50.8 12.3 %prepare.1 = (bf16[32,128,832]{2,1,0:T(8,128)(2,1)}, bf16[32,256,128]{2,1,0:T(8,128)(2,1)}, bf16[8,128,2112]{2,1,0:T(8,128)(2,1)}) custom-call(f32[584,128]{1,0:T(8,128)} %get-tuple-element.45.after, f32[32,64,768]{2,1,0:T(8,128)} %coupling.1, f32[32,64,256]{2,1,0:T(8,128)} %basis.3, f32[32,64,64]{2,1,0:T(8,128)} %transfer.3, f32[8,64,2048]{2,1,0:T(8,128)} %mid_coupling.1, ...), custom_call_target="tpu_custom_call" | custom-call | bytes 30000000 | tf_op jit(solution)/shard_map/prepare/pallas_call | solution.py:245
  63.2 0.0 collective-permute-start.7
  63.2 0.5 collective-permute-start.8
  63.7 0.8 collective-permute-done.7.refs_8_
  64.6 0.1 collective-permute-start.9
  64.7 0.1 collective-permute-done.8.refs_9_
  64.8 0.3 collective-permute-start.10
  65.1 0.9 collective-permute-done.9.refs_10_
  66.0 0.1 collective-permute-start.13
  66.1 0.3 collective-permute-done.10.refs_11_
  66.4 8.4 %collective-permute-done.6.refs_5_ = f32[15,64,128]{2,1,0:T(8,128)S(1)} collective-permute-done((f32[15,64,128]{2,1,0:T(8,128)}, f32[15,64,128]{2,1,0:T(8,128)S(1)}, u32[]{:S(2)}, u32[]{:S(2)}) %collective-permute-start.6) | collective-permute-done | bytes 491552 | tf_op jit(solution)/shard_map/ppermute | solution.py:483
  74.8 3.1 %collective-permute-done.11.refs_6_ = f32[15,64,128]{2,1,0:T(8,128)} collective-permute-done((f32[15,64,128]{2,1,0:T(8,128)}, f32[15,64,128]{2,1,0:T(8,128)}, u32[]{:S(2)}, u32[]{:S(2)}) %collective-permute-start.11) | collective-permute-done | bytes 491552 | tf_op jit(solution)/shard_map/ppermute | solution.py:483
  77.9 0.0 collective-permute-start.15
  77.9 12.2 %collective-permute-done.12.refs_7_ = f32[15,64,128]{2,1,0:T(8,128)} collective-permute-done((f32[15,64,128]{2,1,0:T(8,128)}, f32[15,64,128]{2,1,0:T(8,128)}, u32[]{:S(2)}, u32[]{:S(2)}) %collective-permute-start.12) | collective-permute-done | bytes 491552 | tf_op jit(solution)/shard_map/ppermute | solution.py:483
  90.1 0.0 collective-permute-start.16
  90.1 0.5 collective-permute-start.14
  90.6 0.1 copy.15.pair_leaf
  90.7 0.0 collective-permute-done.13.refs_12_
  90.7 0.0 collective-permute-done.15.refs_14_
  90.7 1.6 %collective-permute-done.16.refs_15_ = f32[15,64,128]{2,1,0:T(8,128)} collective-permute-done((f32[15,64,128]{2,1,0:T(8,128)}, f32[15,64,128]{2,1,0:T(8,128)}, u32[]{:S(2)}, u32[]{:S(2)}) %collective-permute-start.16) | collective-permute-done | bytes 491552 | tf_op jit(solution)/shard_map/ppermute | solution.py:496
  92.3 0.5 collective-permute-done.14.refs_13_
  92.8 1.6 %all-to-all-done.refs_16_ = f32[64,64,128]{2,1,0:T(8,128)S(1)} async-done(((f32[64,64,128]{2,1,0:T(8,128)}), f32[64,64,128]{2,1,0:T(8,128)S(1)}, u32[]{:S(2)}, u32[]{:S(2)}) %all-to-all-start) | async-done | bytes 2097184 | tf_op jit(solution)/shard_map/all_to_all | solution.py:490
  94.4 12.7 %tail.1 = f32[8192,128]{1,0:T(8,128)} custom-call(s32[32]{0:T(128)S(1)} %copy-done.1, s32[8,32]{1,0:T(8,128)S(1)} %fusion.7.pair, s32[1]{0:T(128)} %bitcast.1.lane_at.position, s32[4]{0:T(128)S(1)} %and_select_fusion.3.tops, s32[32]{0:T(128)S(1)} %copy-done.2, s32[32,12]{1,0:T(8,128)S(1)} %copy.15.pair_leaf, f32[5,64,128]{2,1,0:T(8,128)} %get-tuple-element.55.refs_0_, ...), custom_call_target="tpu_custom_call" | custom-call | flops 6000000000 | bytes 20000000 | tf_op jit(solution)/shard_map/tail/pallas_call | solution.py:421
  (33 shorter events, 0.1 us)
Async XLA Ops:
  0.0 50.6 %copy-start = (s32[8,4]{0,1:T(4,128)S(1)}, s32[8,4]{0,1:T(4,128)}, u32[]{:S(2)}) copy-start(s32[8,4]{0,1:T(4,128)} %param.26) | copy-start | bytes 388
  7.4 10.9 %collective-permute-start = (f32[584,128]{1,0:T(8,128)}, f32[584,128]{1,0:T(8,128)S(1)}, u32[]{:S(2)}, u32[]{:S(2)}) collective-permute-start(f32[584,128]{1,0:T(8,128)} %get-tuple-element.45.after), channel_id=1, source_target_pairs={{0,2},{1,3},{2,0},{3,1},{4,6},{5,7},{6,4},{7,5},{8,10},{9,11},{10,... | collective-permute-start | bytes 897032 | tf_op jit(solution)/shard_map/ppermute | solution.py:459
  10.5 17.2 %collective-permute-start.5 = (f32[584,128]{1,0:T(8,128)}, f32[584,128]{1,0:T(8,128)S(1)}, u32[]{:S(2)}, u32[]{:S(2)}) collective-permute-start(f32[584,128]{1,0:T(8,128)} %get-tuple-element.45.after), channel_id=1, source_target_pairs={{0,6},{1,7},{2,4},{3,5},{4,2},{5,3},{6,0},{7,1},{8,14},{9,15},{10,... | collective-permute-start | bytes 897032 | tf_op jit(solution)/shard_map/ppermute | solution.py:459
  13.0 26.4 %collective-permute-start.4 = (f32[584,128]{1,0:T(8,128)}, f32[584,128]{1,0:T(8,128)S(1)}, u32[]{:S(2)}, u32[]{:S(2)}) collective-permute-start(f32[584,128]{1,0:T(8,128)} %get-tuple-element.45.after), channel_id=1, source_target_pairs={{0,4},{1,5},{2,6},{3,7},{4,0},{5,1},{6,2},{7,3},{8,12},{9,13},{10,... | collective-permute-start | bytes 897032 | tf_op jit(solution)/shard_map/ppermute | solution.py:459
  18.3 26.0 %copy-start.5 = (f32[584,128]{1,0:T(8,128)}, f32[584,128]{1,0:T(8,128)S(1)}, u32[]{:S(2)}) copy-start(f32[584,128]{1,0:T(8,128)S(1)} %collective-permute-done.refs_0_) | copy-start | bytes 897028
  18.3 21.1 %collective-permute-start.1 = (f32[5,64,128]{2,1,0:T(8,128)}, f32[5,64,128]{2,1,0:T(8,128)S(1)}, u32[]{:S(2)}, u32[]{:S(2)}) collective-permute-start(f32[5,64,128]{2,1,0:T(8,128)} %get-tuple-element.47), channel_id=1, source_target_pairs={{0,8},{8,0},{16,24},{24,16},{1,9},{9,1},{17,25},{25,17},{2,10},{10... | collective-permute-start | bytes 491528 | tf_op jit(solution)/shard_map/ppermute | solution.py:483
  19.8 19.6 %collective-permute-start.2 = (f32[5,64,128]{2,1,0:T(8,128)}, f32[5,64,128]{2,1,0:T(8,128)S(1)}, u32[]{:S(2)}, u32[]{:S(2)}) collective-permute-start(f32[5,64,128]{2,1,0:T(8,128)} %get-tuple-element.48), channel_id=1, source_target_pairs={{0,16},{8,24},{16,0},{24,8},{1,17},{9,25},{17,1},{25,9},{2,18},{10... | collective-permute-start | bytes 491528 | tf_op jit(solution)/shard_map/ppermute | solution.py:483
  21.3 18.1 %collective-permute-start.3 = (f32[5,64,128]{2,1,0:T(8,128)}, f32[5,64,128]{2,1,0:T(8,128)}, u32[]{:S(2)}, u32[]{:S(2)}) collective-permute-start(f32[5,64,128]{2,1,0:T(8,128)} %get-tuple-element.49), channel_id=1, source_target_pairs={{0,24},{8,16},{16,8},{24,0},{1,25},{9,17},{17,9},{25,1},{2,26},{10... | collective-permute-start | bytes 491528 | tf_op jit(solution)/shard_map/ppermute | solution.py:483
  27.6 16.6 %copy-start.6 = (f32[584,128]{1,0:T(8,128)}, f32[584,128]{1,0:T(8,128)S(1)}, u32[]{:S(2)}) copy-start(f32[584,128]{1,0:T(8,128)S(1)} %collective-permute-done.5.refs_2_) | copy-start | bytes 897028
  39.4 4.9 %copy-start.7 = (f32[584,128]{1,0:T(8,128)}, f32[584,128]{1,0:T(8,128)S(1)}, u32[]{:S(2)}) copy-start(f32[584,128]{1,0:T(8,128)S(1)} %collective-permute-done.4.refs_1_) | copy-start | bytes 897028
  39.4 23.8 %copy-start.9 = (f32[5,64,128]{2,1,0:T(8,128)}, f32[5,64,128]{2,1,0:T(8,128)S(1)}, u32[]{:S(2)}) copy-start(f32[5,64,128]{2,1,0:T(8,128)S(1)} %collective-permute-done.1.refs_1_) | copy-start | bytes 491524
  39.4 7.6 %copy-start.10 = (f32[5,64,128]{2,1,0:T(8,128)}, f32[5,64,128]{2,1,0:T(8,128)S(1)}, u32[]{:S(2)}) copy-start(f32[5,64,128]{2,1,0:T(8,128)S(1)} %collective-permute-done.2.refs_2_) | copy-start | bytes 491524
  39.4 55.0 %all-to-all-start = ((f32[64,64,128]{2,1,0:T(8,128)}), f32[64,64,128]{2,1,0:T(8,128)S(1)}, u32[]{:S(2)}, u32[]{:S(2)}) async-start(f32[64,64,128]{2,1,0:T(8,128)} %spread.1), calls=%async_computation | async-start | bytes 4194304 | tf_op jit(solution)/shard_map/all_to_all | solution.py:490
  47.0 27.8 %collective-permute-start.6 = (f32[15,64,128]{2,1,0:T(8,128)}, f32[15,64,128]{2,1,0:T(8,128)S(1)}, u32[]{:S(2)}, u32[]{:S(2)}) collective-permute-start(f32[15,64,128]{2,1,0:T(8,128)} %get-tuple-element.54), channel_id=1, source_target_pairs={{0,8},{8,0},{16,24},{24,16},{1,9},{9,1},{17,25},{25,17},{2,10},{10... | collective-permute-start | bytes 1474568 | tf_op jit(solution)/shard_map/ppermute | solution.py:483
  48.9 29.0 %collective-permute-start.11 = (f32[15,64,128]{2,1,0:T(8,128)}, f32[15,64,128]{2,1,0:T(8,128)}, u32[]{:S(2)}, u32[]{:S(2)}) collective-permute-start(f32[15,64,128]{2,1,0:T(8,128)} %get-tuple-element.65), channel_id=1, source_target_pairs={{0,16},{8,24},{16,0},{24,8},{1,17},{9,25},{17,1},{25,9},{2,18},{10... | collective-permute-start | bytes 1474568 | tf_op jit(solution)/shard_map/ppermute | solution.py:483
  50.3 39.7 %collective-permute-start.12 = (f32[15,64,128]{2,1,0:T(8,128)}, f32[15,64,128]{2,1,0:T(8,128)}, u32[]{:S(2)}, u32[]{:S(2)}) collective-permute-start(f32[15,64,128]{2,1,0:T(8,128)} %get-tuple-element.66), channel_id=1, source_target_pairs={{0,24},{8,16},{16,8},{24,0},{1,25},{9,17},{17,9},{25,1},{2,26},{10... | collective-permute-start | bytes 1474568 | tf_op jit(solution)/shard_map/ppermute | solution.py:483
  50.8 12.4 %copy-start.8 = (f32[5,64,128]{2,1,0:T(8,128)S(1)}, f32[5,64,128]{2,1,0:T(8,128)}, u32[]{:S(2)}) copy-start(f32[5,64,128]{2,1,0:T(8,128)} %get-tuple-element.55.refs_0_) | copy-start | bytes 491524
  50.8 12.9 %copy-start.17 = (s32[8,32]{1,0:T(8,128)S(1)}, s32[8,32]{1,0:T(8,128)}, u32[]{:S(2)}) copy-start(s32[8,32]{1,0:T(8,128)} %param.24) | copy-start | bytes 3076
  50.8 13.8 %copy-start.11 = (f32[5,64,128]{2,1,0:T(8,128)S(1)}, f32[5,64,128]{2,1,0:T(8,128)}, u32[]{:S(2)}) copy-start(f32[5,64,128]{2,1,0:T(8,128)} %copy-done.10) | copy-start | bytes 491524
  50.8 15.2 %copy-start.3 = (f32[15,64,128]{2,1,0:T(8,128)S(1)}, f32[15,64,128]{2,1,0:T(8,128)}, u32[]{:S(2)}) copy-start(f32[15,64,128]{2,1,0:T(8,128)} %get-tuple-element.63.refs_4_) | copy-start | bytes 1474564
  50.8 39.8 %copy-start.16 = (s32[32,12]{0,1:T(8,128)S(1)}, s32[32,12]{0,1:T(8,128)}, u32[]{:S(2)}) copy-start(s32[32,12]{0,1:T(8,128)} %param.21) | copy-start | bytes 4612
  50.8 43.6 %copy-start.1 = (s32[32]{0:T(128)S(1)}, s32[32]{0:T(128)}, u32[]{:S(2)}) copy-start(s32[32]{0:T(128)} %parent.3) | copy-start | bytes 388
  50.8 43.6 %copy-start.2 = (s32[32]{0:T(128)S(1)}, s32[32]{0:T(128)}, u32[]{:S(2)}) copy-start(s32[32]{0:T(128)} %size.3) | copy-start | bytes 388
  63.2 1.4 %collective-permute-start.7 = (f32[5,64,128]{2,1,0:T(8,128)S(1)}, f32[5,64,128]{2,1,0:T(8,128)S(1)}, u32[]{:S(2)}, u32[]{:S(2)}) collective-permute-start(f32[5,64,128]{2,1,0:T(8,128)S(1)} %copy-done.8), channel_id=1, source_target_pairs={{0,1},{1,0},{2,3},{3,2},{4,5},{5,4},{6,7},{7,6},{8,9},{9,8},{10,11... | collective-permute-start | bytes 491528 | tf_op jit(solution)/shard_map/ppermute | solution.py:491
  63.2 1.6 %collective-permute-start.8 = (f32[5,64,128]{2,1,0:T(8,128)S(1)}, f32[5,64,128]{2,1,0:T(8,128)S(1)}, u32[]{:S(2)}, u32[]{:S(2)}) collective-permute-start(f32[5,64,128]{2,1,0:T(8,128)S(1)} %collective-permute-done.1.refs_1_), channel_id=1, source_target_pairs={{0,1},{1,0},{2,3},{3,2},{4,5},{5,4},{6,7},{7,6},{8,9},{9,8},{10,11... | collective-permute-start | bytes 491528 | tf_op jit(solution)/shard_map/ppermute | solution.py:491
  64.6 25.5 %copy-start.12 = (f32[5,64,128]{2,1,0:T(8,128)}, f32[5,64,128]{2,1,0:T(8,128)S(1)}, u32[]{:S(2)}) copy-start(f32[5,64,128]{2,1,0:T(8,128)S(1)} %collective-permute-done.7.refs_8_) | copy-start | bytes 491524
  64.6 1.4 %collective-permute-start.9 = (f32[5,64,128]{2,1,0:T(8,128)S(1)}, f32[5,64,128]{2,1,0:T(8,128)S(1)}, u32[]{:S(2)}, u32[]{:S(2)}) collective-permute-start(f32[5,64,128]{2,1,0:T(8,128)S(1)} %copy-done.11), channel_id=1, source_target_pairs={{0,1},{1,0},{2,3},{3,2},{4,5},{5,4},{6,7},{7,6},{8,9},{9,8},{10,11... | collective-permute-start | bytes 491528 | tf_op jit(solution)/shard_map/ppermute | solution.py:491
  64.8 25.3 %copy-start.13 = (f32[5,64,128]{2,1,0:T(8,128)}, f32[5,64,128]{2,1,0:T(8,128)S(1)}, u32[]{:S(2)}) copy-start(f32[5,64,128]{2,1,0:T(8,128)S(1)} %collective-permute-done.8.refs_9_) | copy-start | bytes 491524
  64.8 1.6 %collective-permute-start.10 = (f32[5,64,128]{2,1,0:T(8,128)}, f32[5,64,128]{2,1,0:T(8,128)S(1)}, u32[]{:S(2)}, u32[]{:S(2)}) collective-permute-start(f32[5,64,128]{2,1,0:T(8,128)} %collective-permute-done.3.refs_3_), channel_id=1, source_target_pairs={{0,1},{1,0},{2,3},{3,2},{4,5},{5,4},{6,7},{7,6},{8,9},{9,8},{10,11... | collective-permute-start | bytes 491528 | tf_op jit(solution)/shard_map/ppermute | solution.py:491
  66.0 28.4 %copy-start.14 = (f32[5,64,128]{2,1,0:T(8,128)}, f32[5,64,128]{2,1,0:T(8,128)S(1)}, u32[]{:S(2)}) copy-start(f32[5,64,128]{2,1,0:T(8,128)S(1)} %collective-permute-done.9.refs_10_) | copy-start | bytes 491524
  66.0 24.7 %collective-permute-start.13 = (f32[15,64,128]{2,1,0:T(8,128)S(1)}, f32[15,64,128]{2,1,0:T(8,128)}, u32[]{:S(2)}, u32[]{:S(2)}) collective-permute-start(f32[15,64,128]{2,1,0:T(8,128)S(1)} %copy-done.3), channel_id=1, source_target_pairs={{0,1},{1,0},{2,3},{3,2},{4,5},{5,4},{6,7},{7,6},{8,9},{9,8},{10,11... | collective-permute-start | bytes 1474568 | tf_op jit(solution)/shard_map/ppermute | solution.py:496
  66.4 28.0 %copy-start.15 = (f32[5,64,128]{2,1,0:T(8,128)}, f32[5,64,128]{2,1,0:T(8,128)S(1)}, u32[]{:S(2)}) copy-start(f32[5,64,128]{2,1,0:T(8,128)S(1)} %collective-permute-done.10.refs_11_) | copy-start | bytes 491524
  74.8 19.6 %copy-start.4 = (f32[15,64,128]{2,1,0:T(8,128)}, f32[15,64,128]{2,1,0:T(8,128)S(1)}, u32[]{:S(2)}) copy-start(f32[15,64,128]{2,1,0:T(8,128)S(1)} %collective-permute-done.6.refs_5_) | copy-start | bytes 1474564
  77.9 12.8 %collective-permute-start.15 = (f32[15,64,128]{2,1,0:T(8,128)}, f32[15,64,128]{2,1,0:T(8,128)}, u32[]{:S(2)}, u32[]{:S(2)}) collective-permute-start(f32[15,64,128]{2,1,0:T(8,128)} %collective-permute-done.11.refs_6_), channel_id=1, source_target_pairs={{0,1},{1,0},{2,3},{3,2},{4,5},{5,4},{6,7},{7,6},{8,9},{9,8},{10,11... | collective-permute-start | bytes 1474568 | tf_op jit(solution)/shard_map/ppermute | solution.py:496
  90.1 2.2 %collective-permute-start.16 = (f32[15,64,128]{2,1,0:T(8,128)}, f32[15,64,128]{2,1,0:T(8,128)}, u32[]{:S(2)}, u32[]{:S(2)}) collective-permute-start(f32[15,64,128]{2,1,0:T(8,128)} %collective-permute-done.12.refs_7_), channel_id=1, source_target_pairs={{0,1},{1,0},{2,3},{3,2},{4,5},{5,4},{6,7},{7,6},{8,9},{9,8},{10,11... | collective-permute-start | bytes 1474568 | tf_op jit(solution)/shard_map/ppermute | solution.py:496
  90.1 2.7 %collective-permute-start.14 = (f32[15,64,128]{2,1,0:T(8,128)S(1)}, f32[15,64,128]{2,1,0:T(8,128)}, u32[]{:S(2)}, u32[]{:S(2)}) collective-permute-start(f32[15,64,128]{2,1,0:T(8,128)S(1)} %collective-permute-done.6.refs_5_), channel_id=1, source_target_pairs={{0,1},{1,0},{2,3},{3,2},{4,5},{5,4},{6,7},{7,6},{8,9},{9,8},{10,11... | collective-permute-start | bytes 1474568 | tf_op jit(solution)/shard_map/ppermute | solution.py:496

commit v3 on v2

--- a/solution.py
+++ b/solution.py
@@ -113,7 +113,7 @@
     leaves, rank, points = basis.shape
     ports = charges.shape[1]
     mids = mid_transfer.shape[0]
-    group = 8
+    group = 4
     send_mid = slots.reshape(-1, min(slots.shape[0], ports))
     up_rows = (mids + 1) * rank + -(-send_mid.shape[0] // 8) * 8
     message = (2 * sizes[1] + 1, rank, ports)
@@ -329,6 +329,10 @@
         held = held_messages[index]
         first_slot, first_top = (lines_held, 0) if side == 0 else (0, piece)
         fetch_message(index).wait()
+        if index == count:
+            for step in range(ahead):
+                for copy in fetch_leaves(step):
+                    copy.start()
 
         @pl.loop(0, piece, unroll=min(piece, 6))
         def _(slot):
@@ -337,9 +341,6 @@
         for line in range(lines_held):
             top_parts[base + line] = lanes_of(held[first_top + line])
 
-    for index in range(ahead):
-        for copy in fetch_leaves(index):
-            copy.start()
     fetch_top.wait()
     stacked = jnp.concatenate([top_parts[tops[k]] for k in range(tops.shape[0])], axis=0)
     near_top[...] = lanes_of(fold(dot(rows_of(top_held[...]), stacked)))
@@ -394,7 +395,7 @@
     leaves, points, _ = basis.shape
     slots, rank, ports = arrived.shape
     owners = slots // per_pair
-    group, chunk, ahead = 4, min(slots, 32), 3
+    group, chunk, ahead = 4, min(slots, 32), 6
     held = []
     for message in range(len(near_side)):
         batch = message // groups

time: 108 us -> 110 us (1.019)
  Pallas kernels: 37.9 us -> 40.2 us
    pallas_call x1, Pallas kernels: 7.43 us -> 9.79 us  [up_sweep(): pl.pallas_call(functools.partial(up_kernel, sizes), grid_spec=pltpu.Prefe...]
  transfers between devices with their start and end apart: 18 -> 18, of which waited for: 13 -> 13; matrix products, arithmetic and copies ran while one was open for 0% -> 0% of each run, Pallas kernels for 17% -> 16%
where the time goes in v3:
time: 110 us; the launch traced here: 109 us
  waiting for transfers between devices  49.5 us (45%)
  Pallas kernels  40.2 us (37%)
  starting transfers between devices  19.2 us (17%)
    ppermute x6, waiting for transfers between devices, body(): lax.ppermute(messages[d], 'group', [(g, g ^ d) for g in range(groups)])  23.6 us
    ppermute x3, waiting for transfers between devices, body(): lax.ppermute(lifted, 'cluster', [(c, c ^ 2 * d) for c in range(per_cluste...  20 us
    pallas_call x1, Pallas kernels, tail(): pl.pallas_call(functools.partial(tail_kernel, (bounds, per_pair, groups,...  12.7 us
    pallas_call x1, Pallas kernels, prepare(): pl.pallas_call(prepare_kernel, grid=(steps,), in_specs=[pl.BlockSpec(memo...  12.3 us
    pallas_call x1, Pallas kernels, up_sweep(): pl.pallas_call(functools.partial(up_kernel, sizes), grid_spec=pltpu.Prefe...  9.79 us
    ppermute x6, starting transfers between devices, body(): lax.ppermute(messages[d], 'group', [(g, g ^ d) for g in range(groups)])  7.04 us
    ppermute x3, starting transfers between devices, body(): lax.ppermute(lifted, 'cluster', [(c, c ^ 2 * d) for c in range(per_cluste...  5.65 us
    all_to_all x1, starting transfers between devices, body(): lax.all_to_all(outgoing, AXES, split_axis=0, concat_axis=0, tiled=True)  4.88 us
  transfers between devices with their start and end apart: 18, of which 13 were waited for; matrix products, arithmetic and copies ran while one was open for 0% of the time, Pallas kernels for 16%

profile of v3, /device:TPU:0, one launch (start us, length us, event | category | flops | bytes accessed | tf_op | source)
XLA Modules:
  0.0 109.5 jit_solution(16264685095870678362)
XLA Ops:
  0.0 0.0 copy-start
  0.0 9.8 %up_sweep.1 = (f32[32,64,128]{2,1,0:T(8,128)}, f32[584,128]{1,0:T(8,128)}, f32[5,64,128]{2,1,0:T(8,128)}, f32[5,64,128]{2,1,0:T(8,128)}, f32[5,64,128]{2,1,0:T(8,128)}, /*index=5*/f32[5,64,128]{2,1,0:T(8,128)}) custom-call(s32[32]{0:T(128)} %size.3, s32[32]{0:T(128)} %parent.3, s32[64]{0:T(128)} %slots.1, s32[1]{0:T(128)} %bitcast.group_at, ...), custom_call_target="tpu_custom_call" | custom-call | flops 1000000000 | bytes 10000000 | tf_op jit(solution)/shard_map/up_sweep/pallas_call | solution.py:120
  9.8 3.1 %collective-permute-start = (f32[584,128]{1,0:T(8,128)}, f32[584,128]{1,0:T(8,128)S(1)}, u32[]{:S(2)}, u32[]{:S(2)}) collective-permute-start(f32[584,128]{1,0:T(8,128)} %get-tuple-element.45.after), channel_id=1, source_target_pairs={{0,2},{1,3},{2,0},{3,1},{4,6},{5,7},{6,4},{7,5},{8,10},{9,11},{10,... | collective-permute-start | bytes 897032 | tf_op jit(solution)/shard_map/ppermute | solution.py:460
  12.9 2.5 %collective-permute-start.5 = (f32[584,128]{1,0:T(8,128)}, f32[584,128]{1,0:T(8,128)S(1)}, u32[]{:S(2)}, u32[]{:S(2)}) collective-permute-start(f32[584,128]{1,0:T(8,128)} %get-tuple-element.45.after), channel_id=1, source_target_pairs={{0,6},{1,7},{2,4},{3,5},{4,2},{5,3},{6,0},{7,1},{8,14},{9,15},{10,... | collective-permute-start | bytes 897032 | tf_op jit(solution)/shard_map/ppermute | solution.py:460
  15.3 0.1 collective-permute-start.4
  15.4 5.2 %collective-permute-done.refs_0_ = f32[584,128]{1,0:T(8,128)S(1)} collective-permute-done((f32[584,128]{1,0:T(8,128)}, f32[584,128]{1,0:T(8,128)S(1)}, u32[]{:S(2)}, u32[]{:S(2)}) %collective-permute-start) | collective-permute-done | bytes 299040 | tf_op jit(solution)/shard_map/ppermute | solution.py:460
  20.7 1.5 %collective-permute-start.1 = (f32[5,64,128]{2,1,0:T(8,128)}, f32[5,64,128]{2,1,0:T(8,128)S(1)}, u32[]{:S(2)}, u32[]{:S(2)}) collective-permute-start(f32[5,64,128]{2,1,0:T(8,128)} %get-tuple-element.47), channel_id=1, source_target_pairs={{0,8},{8,0},{16,24},{24,16},{1,9},{9,1},{17,25},{25,17},{2,10},{10... | collective-permute-start | bytes 491528 | tf_op jit(solution)/shard_map/ppermute | solution.py:484
  22.2 1.5 %collective-permute-start.2 = (f32[5,64,128]{2,1,0:T(8,128)}, f32[5,64,128]{2,1,0:T(8,128)S(1)}, u32[]{:S(2)}, u32[]{:S(2)}) collective-permute-start(f32[5,64,128]{2,1,0:T(8,128)} %get-tuple-element.48), channel_id=1, source_target_pairs={{0,16},{8,24},{16,0},{24,8},{1,17},{9,25},{17,1},{25,9},{2,18},{10... | collective-permute-start | bytes 491528 | tf_op jit(solution)/shard_map/ppermute | solution.py:484
  23.7 0.5 collective-permute-start.3
  24.2 2.7 %spread.1 = f32[64,64,128]{2,1,0:T(8,128)} custom-call(s32[64]{0:T(128)} %send.1, f32[32,64,128]{2,1,0:T(8,128)} %get-tuple-element.40.coef), custom_call_target="tpu_custom_call" | custom-call | bytes 4000000 | tf_op jit(solution)/shard_map/spread/pallas_call | solution.py:158
  26.9 3.1 %collective-permute-done.5.refs_2_ = f32[584,128]{1,0:T(8,128)S(1)} collective-permute-done((f32[584,128]{1,0:T(8,128)}, f32[584,128]{1,0:T(8,128)S(1)}, u32[]{:S(2)}, u32[]{:S(2)}) %collective-permute-start.5) | collective-permute-done | bytes 299040 | tf_op jit(solution)/shard_map/ppermute | solution.py:460
  30.0 11.7 %collective-permute-done.4.refs_1_ = f32[584,128]{1,0:T(8,128)S(1)} collective-permute-done((f32[584,128]{1,0:T(8,128)}, f32[584,128]{1,0:T(8,128)S(1)}, u32[]{:S(2)}, u32[]{:S(2)}) %collective-permute-start.4) | collective-permute-done | bytes 299040 | tf_op jit(solution)/shard_map/ppermute | solution.py:460
  41.7 0.0 collective-permute-done.1.refs_1_
  41.7 0.0 collective-permute-done.2.refs_2_
  41.7 0.0 collective-permute-done.3.refs_3_
  41.8 4.9 %all-to-all-start = ((f32[64,64,128]{2,1,0:T(8,128)}), f32[64,64,128]{2,1,0:T(8,128)S(1)}, u32[]{:S(2)}, u32[]{:S(2)}) async-start(f32[64,64,128]{2,1,0:T(8,128)} %spread.1), calls=%async_computation | async-start | bytes 4194304 | tf_op jit(solution)/shard_map/all_to_all | solution.py:491
  46.7 2.7 %select.31 = (f32[15,64,128]{2,1,0:T(8,128)}, f32[15,64,128]{2,1,0:T(8,128)}, f32[15,64,128]{2,1,0:T(8,128)}, f32[15,64,128]{2,1,0:T(8,128)}) custom-call(s32[1]{0:T(128)} %bitcast.group_at, s32[1]{0:T(128)} %bitcast.1.lane_at.position, f32[584,128]{1,0:T(8,128)} %copy-done.5, f32[584,128]{1,0:T(8,128)} %copy-done.7, f32[584,128]{1,0:T(8,128)} %copy-done.6), custom_call_target="tpu_custom_call" | custom-call | bytes 4000000 | tf_op jit(solution)/shard_map/select/pallas_call | solution.py:208
  49.4 1.8 %collective-permute-start.6 = (f32[15,64,128]{2,1,0:T(8,128)}, f32[15,64,128]{2,1,0:T(8,128)S(1)}, u32[]{:S(2)}, u32[]{:S(2)}) collective-permute-start(f32[15,64,128]{2,1,0:T(8,128)} %get-tuple-element.54), channel_id=1, source_target_pairs={{0,8},{8,0},{16,24},{24,16},{1,9},{9,1},{17,25},{25,17},{2,10},{10... | collective-permute-start | bytes 1474568 | tf_op jit(solution)/shard_map/ppermute | solution.py:484
  51.2 1.5 %collective-permute-start.11 = (f32[15,64,128]{2,1,0:T(8,128)}, f32[15,64,128]{2,1,0:T(8,128)}, u32[]{:S(2)}, u32[]{:S(2)}) collective-permute-start(f32[15,64,128]{2,1,0:T(8,128)} %get-tuple-element.65), channel_id=1, source_target_pairs={{0,16},{8,24},{16,0},{24,8},{1,17},{9,25},{17,1},{25,9},{2,18},{10... | collective-permute-start | bytes 1474568 | tf_op jit(solution)/shard_map/ppermute | solution.py:484
  52.7 0.3 collective-permute-start.12
  53.0 0.2 dynamic-slice_reduce_fusion
  53.1 0.0 copy-start.17
  53.2 0.0 copy-start.16
  53.2 0.0 copy-start.1
  53.2 0.0 copy-start.2
  53.2 12.3 %prepare.1 = (bf16[32,128,832]{2,1,0:T(8,128)(2,1)}, bf16[32,256,128]{2,1,0:T(8,128)(2,1)}, bf16[8,128,2112]{2,1,0:T(8,128)(2,1)}) custom-call(f32[584,128]{1,0:T(8,128)} %get-tuple-element.45.after, f32[32,64,768]{2,1,0:T(8,128)} %coupling.1, f32[32,64,256]{2,1,0:T(8,128)} %basis.3, f32[32,64,64]{2,1,0:T(8,128)} %transfer.3, f32[8,64,2048]{2,1,0:T(8,128)} %mid_coupling.1, ...), custom_call_target="tpu_custom_call" | custom-call | bytes 30000000 | tf_op jit(solution)/shard_map/prepare/pallas_call | solution.py:245
  65.5 0.0 collective-permute-start.7
  65.6 0.5 collective-permute-start.8
  66.1 0.8 collective-permute-done.7.refs_8_
  66.9 0.1 collective-permute-start.9
  67.1 0.1 collective-permute-done.8.refs_9_
  67.2 0.3 collective-permute-start.10
  67.5 0.9 collective-permute-done.9.refs_10_
  68.3 0.1 collective-permute-start.13
  68.5 0.3 collective-permute-done.10.refs_11_
  68.8 8.4 %collective-permute-done.6.refs_5_ = f32[15,64,128]{2,1,0:T(8,128)S(1)} collective-permute-done((f32[15,64,128]{2,1,0:T(8,128)}, f32[15,64,128]{2,1,0:T(8,128)S(1)}, u32[]{:S(2)}, u32[]{:S(2)}) %collective-permute-start.6) | collective-permute-done | bytes 491552 | tf_op jit(solution)/shard_map/ppermute | solution.py:484
  77.2 3.1 %collective-permute-done.11.refs_6_ = f32[15,64,128]{2,1,0:T(8,128)} collective-permute-done((f32[15,64,128]{2,1,0:T(8,128)}, f32[15,64,128]{2,1,0:T(8,128)}, u32[]{:S(2)}, u32[]{:S(2)}) %collective-permute-start.11) | collective-permute-done | bytes 491552 | tf_op jit(solution)/shard_map/ppermute | solution.py:484
  80.2 0.0 collective-permute-start.15
  80.2 12.2 %collective-permute-done.12.refs_7_ = f32[15,64,128]{2,1,0:T(8,128)} collective-permute-done((f32[15,64,128]{2,1,0:T(8,128)}, f32[15,64,128]{2,1,0:T(8,128)}, u32[]{:S(2)}, u32[]{:S(2)}) %collective-permute-start.12) | collective-permute-done | bytes 491552 | tf_op jit(solution)/shard_map/ppermute | solution.py:484
  92.4 0.0 collective-permute-start.16
  92.4 0.5 collective-permute-start.14
  92.9 0.1 copy.15.pair_leaf
  93.0 0.0 collective-permute-done.13.refs_12_
  93.0 0.0 collective-permute-done.15.refs_14_
  93.0 1.6 %collective-permute-done.16.refs_15_ = f32[15,64,128]{2,1,0:T(8,128)} collective-permute-done((f32[15,64,128]{2,1,0:T(8,128)}, f32[15,64,128]{2,1,0:T(8,128)}, u32[]{:S(2)}, u32[]{:S(2)}) %collective-permute-start.16) | collective-permute-done | bytes 491552 | tf_op jit(solution)/shard_map/ppermute | solution.py:497
  94.6 0.5 collective-permute-done.14.refs_13_
  95.1 1.6 %all-to-all-done.refs_16_ = f32[64,64,128]{2,1,0:T(8,128)S(1)} async-done(((f32[64,64,128]{2,1,0:T(8,128)}), f32[64,64,128]{2,1,0:T(8,128)S(1)}, u32[]{:S(2)}, u32[]{:S(2)}) %all-to-all-start) | async-done | bytes 2097184 | tf_op jit(solution)/shard_map/all_to_all | solution.py:491
  96.8 12.7 %tail.1 = f32[8192,128]{1,0:T(8,128)} custom-call(s32[32]{0:T(128)S(1)} %copy-done.1, s32[8,32]{1,0:T(8,128)S(1)} %fusion.7.pair, s32[1]{0:T(128)} %bitcast.1.lane_at.position, s32[4]{0:T(128)S(1)} %and_select_fusion.3.tops, s32[32]{0:T(128)S(1)} %copy-done.2, s32[32,12]{1,0:T(8,128)S(1)} %copy.15.pair_leaf, f32[5,64,128]{2,1,0:T(8,128)} %get-tuple-element.55.refs_0_, ...), custom_call_target="tpu_custom_call" | custom-call | flops 6000000000 | bytes 20000000 | tf_op jit(solution)/shard_map/tail/pallas_call | solution.py:422
  (33 shorter events, 0.1 us)
Async XLA Ops:
  0.0 53.0 %copy-start = (s32[8,4]{0,1:T(4,128)S(1)}, s32[8,4]{0,1:T(4,128)}, u32[]{:S(2)}) copy-start(s32[8,4]{0,1:T(4,128)} %param.26) | copy-start | bytes 388
  9.8 10.9 %collective-permute-start = (f32[584,128]{1,0:T(8,128)}, f32[584,128]{1,0:T(8,128)S(1)}, u32[]{:S(2)}, u32[]{:S(2)}) collective-permute-start(f32[584,128]{1,0:T(8,128)} %get-tuple-element.45.after), channel_id=1, source_target_pairs={{0,2},{1,3},{2,0},{3,1},{4,6},{5,7},{6,4},{7,5},{8,10},{9,11},{10,... | collective-permute-start | bytes 897032 | tf_op jit(solution)/shard_map/ppermute | solution.py:460
  12.9 17.2 %collective-permute-start.5 = (f32[584,128]{1,0:T(8,128)}, f32[584,128]{1,0:T(8,128)S(1)}, u32[]{:S(2)}, u32[]{:S(2)}) collective-permute-start(f32[584,128]{1,0:T(8,128)} %get-tuple-element.45.after), channel_id=1, source_target_pairs={{0,6},{1,7},{2,4},{3,5},{4,2},{5,3},{6,0},{7,1},{8,14},{9,15},{10,... | collective-permute-start | bytes 897032 | tf_op jit(solution)/shard_map/ppermute | solution.py:460
  15.3 26.4 %collective-permute-start.4 = (f32[584,128]{1,0:T(8,128)}, f32[584,128]{1,0:T(8,128)S(1)}, u32[]{:S(2)}, u32[]{:S(2)}) collective-permute-start(f32[584,128]{1,0:T(8,128)} %get-tuple-element.45.after), channel_id=1, source_target_pairs={{0,4},{1,5},{2,6},{3,7},{4,0},{5,1},{6,2},{7,3},{8,12},{9,13},{10,... | collective-permute-start | bytes 897032 | tf_op jit(solution)/shard_map/ppermute | solution.py:460
  20.7 26.0 %copy-start.5 = (f32[584,128]{1,0:T(8,128)}, f32[584,128]{1,0:T(8,128)S(1)}, u32[]{:S(2)}) copy-start(f32[584,128]{1,0:T(8,128)S(1)} %collective-permute-done.refs_0_) | copy-start | bytes 897028
  20.7 21.1 %collective-permute-start.1 = (f32[5,64,128]{2,1,0:T(8,128)}, f32[5,64,128]{2,1,0:T(8,128)S(1)}, u32[]{:S(2)}, u32[]{:S(2)}) collective-permute-start(f32[5,64,128]{2,1,0:T(8,128)} %get-tuple-element.47), channel_id=1, source_target_pairs={{0,8},{8,0},{16,24},{24,16},{1,9},{9,1},{17,25},{25,17},{2,10},{10... | collective-permute-start | bytes 491528 | tf_op jit(solution)/shard_map/ppermute | solution.py:484
  22.2 19.6 %collective-permute-start.2 = (f32[5,64,128]{2,1,0:T(8,128)}, f32[5,64,128]{2,1,0:T(8,128)S(1)}, u32[]{:S(2)}, u32[]{:S(2)}) collective-permute-start(f32[5,64,128]{2,1,0:T(8,128)} %get-tuple-element.48), channel_id=1, source_target_pairs={{0,16},{8,24},{16,0},{24,8},{1,17},{9,25},{17,1},{25,9},{2,18},{10... | collective-permute-start | bytes 491528 | tf_op jit(solution)/shard_map/ppermute | solution.py:484
  23.7 18.1 %collective-permute-start.3 = (f32[5,64,128]{2,1,0:T(8,128)}, f32[5,64,128]{2,1,0:T(8,128)}, u32[]{:S(2)}, u32[]{:S(2)}) collective-permute-start(f32[5,64,128]{2,1,0:T(8,128)} %get-tuple-element.49), channel_id=1, source_target_pairs={{0,24},{8,16},{16,8},{24,0},{1,25},{9,17},{17,9},{25,1},{2,26},{10... | collective-permute-start | bytes 491528 | tf_op jit(solution)/shard_map/ppermute | solution.py:484
  30.0 16.6 %copy-start.6 = (f32[584,128]{1,0:T(8,128)}, f32[584,128]{1,0:T(8,128)S(1)}, u32[]{:S(2)}) copy-start(f32[584,128]{1,0:T(8,128)S(1)} %collective-permute-done.5.refs_2_) | copy-start | bytes 897028
  41.7 4.9 %copy-start.7 = (f32[584,128]{1,0:T(8,128)}, f32[584,128]{1,0:T(8,128)S(1)}, u32[]{:S(2)}) copy-start(f32[584,128]{1,0:T(8,128)S(1)} %collective-permute-done.4.refs_1_) | copy-start | bytes 897028
  41.7 23.8 %copy-start.9 = (f32[5,64,128]{2,1,0:T(8,128)}, f32[5,64,128]{2,1,0:T(8,128)S(1)}, u32[]{:S(2)}) copy-start(f32[5,64,128]{2,1,0:T(8,128)S(1)} %collective-permute-done.1.refs_1_) | copy-start | bytes 491524
  41.7 7.7 %copy-start.10 = (f32[5,64,128]{2,1,0:T(8,128)}, f32[5,64,128]{2,1,0:T(8,128)S(1)}, u32[]{:S(2)}) copy-start(f32[5,64,128]{2,1,0:T(8,128)S(1)} %collective-permute-done.2.refs_2_) | copy-start | bytes 491524
  41.8 55.0 %all-to-all-start = ((f32[64,64,128]{2,1,0:T(8,128)}), f32[64,64,128]{2,1,0:T(8,128)S(1)}, u32[]{:S(2)}, u32[]{:S(2)}) async-start(f32[64,64,128]{2,1,0:T(8,128)} %spread.1), calls=%async_computation | async-start | bytes 4194304 | tf_op jit(solution)/shard_map/all_to_all | solution.py:491
  49.4 27.8 %collective-permute-start.6 = (f32[15,64,128]{2,1,0:T(8,128)}, f32[15,64,128]{2,1,0:T(8,128)S(1)}, u32[]{:S(2)}, u32[]{:S(2)}) collective-permute-start(f32[15,64,128]{2,1,0:T(8,128)} %get-tuple-element.54), channel_id=1, source_target_pairs={{0,8},{8,0},{16,24},{24,16},{1,9},{9,1},{17,25},{25,17},{2,10},{10... | collective-permute-start | bytes 1474568 | tf_op jit(solution)/shard_map/ppermute | solution.py:484
  51.2 29.0 %collective-permute-start.11 = (f32[15,64,128]{2,1,0:T(8,128)}, f32[15,64,128]{2,1,0:T(8,128)}, u32[]{:S(2)}, u32[]{:S(2)}) collective-permute-start(f32[15,64,128]{2,1,0:T(8,128)} %get-tuple-element.65), channel_id=1, source_target_pairs={{0,16},{8,24},{16,0},{24,8},{1,17},{9,25},{17,1},{25,9},{2,18},{10... | collective-permute-start | bytes 1474568 | tf_op jit(solution)/shard_map/ppermute | solution.py:484
  52.7 39.7 %collective-permute-start.12 = (f32[15,64,128]{2,1,0:T(8,128)}, f32[15,64,128]{2,1,0:T(8,128)}, u32[]{:S(2)}, u32[]{:S(2)}) collective-permute-start(f32[15,64,128]{2,1,0:T(8,128)} %get-tuple-element.66), channel_id=1, source_target_pairs={{0,24},{8,16},{16,8},{24,0},{1,25},{9,17},{17,9},{25,1},{2,26},{10... | collective-permute-start | bytes 1474568 | tf_op jit(solution)/shard_map/ppermute | solution.py:484
  53.1 12.4 %copy-start.8 = (f32[5,64,128]{2,1,0:T(8,128)S(1)}, f32[5,64,128]{2,1,0:T(8,128)}, u32[]{:S(2)}) copy-start(f32[5,64,128]{2,1,0:T(8,128)} %get-tuple-element.55.refs_0_) | copy-start | bytes 491524
  53.1 12.9 %copy-start.17 = (s32[8,32]{1,0:T(8,128)S(1)}, s32[8,32]{1,0:T(8,128)}, u32[]{:S(2)}) copy-start(s32[8,32]{1,0:T(8,128)} %param.24) | copy-start | bytes 3076
  53.2 13.8 %copy-start.11 = (f32[5,64,128]{2,1,0:T(8,128)S(1)}, f32[5,64,128]{2,1,0:T(8,128)}, u32[]{:S(2)}) copy-start(f32[5,64,128]{2,1,0:T(8,128)} %copy-done.10) | copy-start | bytes 491524
  53.2 15.2 %copy-start.3 = (f32[15,64,128]{2,1,0:T(8,128)S(1)}, f32[15,64,128]{2,1,0:T(8,128)}, u32[]{:S(2)}) copy-start(f32[15,64,128]{2,1,0:T(8,128)} %get-tuple-element.63.refs_4_) | copy-start | bytes 1474564
  53.2 39.8 %copy-start.16 = (s32[32,12]{0,1:T(8,128)S(1)}, s32[32,12]{0,1:T(8,128)}, u32[]{:S(2)}) copy-start(s32[32,12]{0,1:T(8,128)} %param.21) | copy-start | bytes 4612
  53.2 43.6 %copy-start.1 = (s32[32]{0:T(128)S(1)}, s32[32]{0:T(128)}, u32[]{:S(2)}) copy-start(s32[32]{0:T(128)} %parent.3) | copy-start | bytes 388
  53.2 43.6 %copy-start.2 = (s32[32]{0:T(128)S(1)}, s32[32]{0:T(128)}, u32[]{:S(2)}) copy-start(s32[32]{0:T(128)} %size.3) | copy-start | bytes 388
  65.5 1.4 %collective-permute-start.7 = (f32[5,64,128]{2,1,0:T(8,128)S(1)}, f32[5,64,128]{2,1,0:T(8,128)S(1)}, u32[]{:S(2)}, u32[]{:S(2)}) collective-permute-start(f32[5,64,128]{2,1,0:T(8,128)S(1)} %copy-done.8), channel_id=1, source_target_pairs={{0,1},{1,0},{2,3},{3,2},{4,5},{5,4},{6,7},{7,6},{8,9},{9,8},{10,11... | collective-permute-start | bytes 491528 | tf_op jit(solution)/shard_map/ppermute | solution.py:492
  65.6 1.6 %collective-permute-start.8 = (f32[5,64,128]{2,1,0:T(8,128)S(1)}, f32[5,64,128]{2,1,0:T(8,128)S(1)}, u32[]{:S(2)}, u32[]{:S(2)}) collective-permute-start(f32[5,64,128]{2,1,0:T(8,128)S(1)} %collective-permute-done.1.refs_1_), channel_id=1, source_target_pairs={{0,1},{1,0},{2,3},{3,2},{4,5},{5,4},{6,7},{7,6},{8,9},{9,8},{10,11... | collective-permute-start | bytes 491528 | tf_op jit(solution)/shard_map/ppermute | solution.py:492
  66.9 25.5 %copy-start.12 = (f32[5,64,128]{2,1,0:T(8,128)}, f32[5,64,128]{2,1,0:T(8,128)S(1)}, u32[]{:S(2)}) copy-start(f32[5,64,128]{2,1,0:T(8,128)S(1)} %collective-permute-done.7.refs_8_) | copy-start | bytes 491524
  66.9 1.4 %collective-permute-start.9 = (f32[5,64,128]{2,1,0:T(8,128)S(1)}, f32[5,64,128]{2,1,0:T(8,128)S(1)}, u32[]{:S(2)}, u32[]{:S(2)}) collective-permute-start(f32[5,64,128]{2,1,0:T(8,128)S(1)} %copy-done.11), channel_id=1, source_target_pairs={{0,1},{1,0},{2,3},{3,2},{4,5},{5,4},{6,7},{7,6},{8,9},{9,8},{10,11... | collective-permute-start | bytes 491528 | tf_op jit(solution)/shard_map/ppermute | solution.py:492
  67.2 25.3 %copy-start.13 = (f32[5,64,128]{2,1,0:T(8,128)}, f32[5,64,128]{2,1,0:T(8,128)S(1)}, u32[]{:S(2)}) copy-start(f32[5,64,128]{2,1,0:T(8,128)S(1)} %collective-permute-done.8.refs_9_) | copy-start | bytes 491524
  67.2 1.6 %collective-permute-start.10 = (f32[5,64,128]{2,1,0:T(8,128)}, f32[5,64,128]{2,1,0:T(8,128)S(1)}, u32[]{:S(2)}, u32[]{:S(2)}) collective-permute-start(f32[5,64,128]{2,1,0:T(8,128)} %collective-permute-done.3.refs_3_), channel_id=1, source_target_pairs={{0,1},{1,0},{2,3},{3,2},{4,5},{5,4},{6,7},{7,6},{8,9},{9,8},{10,11... | collective-permute-start | bytes 491528 | tf_op jit(solution)/shard_map/ppermute | solution.py:492
  68.3 28.4 %copy-start.14 = (f32[5,64,128]{2,1,0:T(8,128)}, f32[5,64,128]{2,1,0:T(8,128)S(1)}, u32[]{:S(2)}) copy-start(f32[5,64,128]{2,1,0:T(8,128)S(1)} %collective-permute-done.9.refs_10_) | copy-start | bytes 491524
  68.3 24.7 %collective-permute-start.13 = (f32[15,64,128]{2,1,0:T(8,128)S(1)}, f32[15,64,128]{2,1,0:T(8,128)}, u32[]{:S(2)}, u32[]{:S(2)}) collective-permute-start(f32[15,64,128]{2,1,0:T(8,128)S(1)} %copy-done.3), channel_id=1, source_target_pairs={{0,1},{1,0},{2,3},{3,2},{4,5},{5,4},{6,7},{7,6},{8,9},{9,8},{10,11... | collective-permute-start | bytes 1474568 | tf_op jit(solution)/shard_map/ppermute | solution.py:497
  68.8 28.0 %copy-start.15 = (f32[5,64,128]{2,1,0:T(8,128)}, f32[5,64,128]{2,1,0:T(8,128)S(1)}, u32[]{:S(2)}) copy-start(f32[5,64,128]{2,1,0:T(8,128)S(1)} %collective-permute-done.10.refs_11_) | copy-start | bytes 491524
  77.2 19.6 %copy-start.4 = (f32[15,64,128]{2,1,0:T(8,128)}, f32[15,64,128]{2,1,0:T(8,128)S(1)}, u32[]{:S(2)}) copy-start(f32[15,64,128]{2,1,0:T(8,128)S(1)} %collective-permute-done.6.refs_5_) | copy-start | bytes 1474564
  80.2 12.8 %collective-permute-start.15 = (f32[15,64,128]{2,1,0:T(8,128)}, f32[15,64,128]{2,1,0:T(8,128)}, u32[]{:S(2)}, u32[]{:S(2)}) collective-permute-start(f32[15,64,128]{2,1,0:T(8,128)} %collective-permute-done.11.refs_6_), channel_id=1, source_target_pairs={{0,1},{1,0},{2,3},{3,2},{4,5},{5,4},{6,7},{7,6},{8,9},{9,8},{10,11... | collective-permute-start | bytes 1474568 | tf_op jit(solution)/shard_map/ppermute | solution.py:497
  92.4 2.2 %collective-permute-start.16 = (f32[15,64,128]{2,1,0:T(8,128)}, f32[15,64,128]{2,1,0:T(8,128)}, u32[]{:S(2)}, u32[]{:S(2)}) collective-permute-start(f32[15,64,128]{2,1,0:T(8,128)} %collective-permute-done.12.refs_7_), channel_id=1, source_target_pairs={{0,1},{1,0},{2,3},{3,2},{4,5},{5,4},{6,7},{7,6},{8,9},{9,8},{10,11... | collective-permute-start | bytes 1474568 | tf_op jit(solution)/shard_map/ppermute | solution.py:497
  92.4 2.7 %collective-permute-start.14 = (f32[15,64,128]{2,1,0:T(8,128)S(1)}, f32[15,64,128]{2,1,0:T(8,128)}, u32[]{:S(2)}, u32[]{:S(2)}) collective-permute-start(f32[15,64,128]{2,1,0:T(8,128)S(1)} %collective-permute-done.6.refs_5_), channel_id=1, source_target_pairs={{0,1},{1,0},{2,3},{3,2},{4,5},{5,4},{6,7},{7,6},{8,9},{9,8},{10,11... | collective-permute-start | bytes 1474568 | tf_op jit(solution)/shard_map/ppermute | solution.py:497

commit v4 on v3

--- a/solution.py
+++ b/solution.py
@@ -113,7 +113,7 @@
     leaves, rank, points = basis.shape
     ports = charges.shape[1]
     mids = mid_transfer.shape[0]
-    group = 4
+    group = 16
     send_mid = slots.reshape(-1, min(slots.shape[0], ports))
     up_rows = (mids + 1) * rank + -(-send_mid.shape[0] // 8) * 8
     message = (2 * sizes[1] + 1, rank, ports)

time: 110 us -> 108 us (0.982)
  Pallas kernels: 40.2 us -> 37.8 us
    pallas_call x1, Pallas kernels: 9.79 us -> 7.38 us  [up_sweep(): pl.pallas_call(functools.partial(up_kernel, sizes), grid_spec=pltpu.Prefe...]
  transfers between devices with their start and end apart: 18 -> 18, of which waited for: 13 -> 13; matrix products, arithmetic and copies ran while one was open for 0% -> 0% of each run, Pallas kernels for 16% -> 17%
where the time goes in v4:
time: 108 us; the launch traced here: 107 us
  waiting for transfers between devices  49.5 us (46%)
  Pallas kernels  37.8 us (35%)
  starting transfers between devices  19.2 us (18%)
    ppermute x6, waiting for transfers between devices, body(): lax.ppermute(messages[d], 'group', [(g, g ^ d) for g in range(groups)])  23.6 us
    ppermute x3, waiting for transfers between devices, body(): lax.ppermute(lifted, 'cluster', [(c, c ^ 2 * d) for c in range(per_cluste...  20 us
    pallas_call x1, Pallas kernels, tail(): pl.pallas_call(functools.partial(tail_kernel, (bounds, per_pair, groups,...  12.7 us
    pallas_call x1, Pallas kernels, prepare(): pl.pallas_call(prepare_kernel, grid=(steps,), in_specs=[pl.BlockSpec(memo...  12.3 us
    pallas_call x1, Pallas kernels, up_sweep(): pl.pallas_call(functools.partial(up_kernel, sizes), grid_spec=pltpu.Prefe...  7.38 us
    ppermute x6, starting transfers between devices, body(): lax.ppermute(messages[d], 'group', [(g, g ^ d) for g in range(groups)])  7.04 us
    ppermute x3, starting transfers between devices, body(): lax.ppermute(lifted, 'cluster', [(c, c ^ 2 * d) for c in range(per_cluste...  5.69 us
    all_to_all x1, starting transfers between devices, body(): lax.all_to_all(outgoing, AXES, split_axis=0, concat_axis=0, tiled=True)  4.88 us
  transfers between devices with their start and end apart: 18, of which 13 were waited for; matrix products, arithmetic and copies ran while one was open for 0% of the time, Pallas kernels for 17%

profile of v4, /device:TPU:0, one launch (start us, length us, event | category | flops | bytes accessed | tf_op | source)
XLA Modules:
  0.0 107.1 jit_solution(16675570918197767233)
XLA Ops:
  0.0 0.0 copy-start
  0.0 7.4 %up_sweep.1 = (f32[32,64,128]{2,1,0:T(8,128)}, f32[584,128]{1,0:T(8,128)}, f32[5,64,128]{2,1,0:T(8,128)}, f32[5,64,128]{2,1,0:T(8,128)}, f32[5,64,128]{2,1,0:T(8,128)}, /*index=5*/f32[5,64,128]{2,1,0:T(8,128)}) custom-call(s32[32]{0:T(128)} %size.3, s32[32]{0:T(128)} %parent.3, s32[64]{0:T(128)} %slots.1, s32[1]{0:T(128)} %bitcast.group_at, ...), custom_call_target="tpu_custom_call" | custom-call | flops 1000000000 | bytes 10000000 | tf_op jit(solution)/shard_map/up_sweep/pallas_call | solution.py:120
  7.4 3.1 %collective-permute-start = (f32[584,128]{1,0:T(8,128)}, f32[584,128]{1,0:T(8,128)S(1)}, u32[]{:S(2)}, u32[]{:S(2)}) collective-permute-start(f32[584,128]{1,0:T(8,128)} %get-tuple-element.45.after), channel_id=1, source_target_pairs={{0,2},{1,3},{2,0},{3,1},{4,6},{5,7},{6,4},{7,5},{8,10},{9,11},{10,... | collective-permute-start | bytes 897032 | tf_op jit(solution)/shard_map/ppermute | solution.py:460
  10.5 2.5 %collective-permute-start.5 = (f32[584,128]{1,0:T(8,128)}, f32[584,128]{1,0:T(8,128)S(1)}, u32[]{:S(2)}, u32[]{:S(2)}) collective-permute-start(f32[584,128]{1,0:T(8,128)} %get-tuple-element.45.after), channel_id=1, source_target_pairs={{0,6},{1,7},{2,4},{3,5},{4,2},{5,3},{6,0},{7,1},{8,14},{9,15},{10,... | collective-permute-start | bytes 897032 | tf_op jit(solution)/shard_map/ppermute | solution.py:460
  12.9 0.1 collective-permute-start.4
  13.1 5.2 %collective-permute-done.refs_0_ = f32[584,128]{1,0:T(8,128)S(1)} collective-permute-done((f32[584,128]{1,0:T(8,128)}, f32[584,128]{1,0:T(8,128)S(1)}, u32[]{:S(2)}, u32[]{:S(2)}) %collective-permute-start) | collective-permute-done | bytes 299040 | tf_op jit(solution)/shard_map/ppermute | solution.py:460
  18.3 1.5 %collective-permute-start.1 = (f32[5,64,128]{2,1,0:T(8,128)}, f32[5,64,128]{2,1,0:T(8,128)S(1)}, u32[]{:S(2)}, u32[]{:S(2)}) collective-permute-start(f32[5,64,128]{2,1,0:T(8,128)} %get-tuple-element.47), channel_id=1, source_target_pairs={{0,8},{8,0},{16,24},{24,16},{1,9},{9,1},{17,25},{25,17},{2,10},{10... | collective-permute-start | bytes 491528 | tf_op jit(solution)/shard_map/ppermute | solution.py:484
  19.8 1.5 %collective-permute-start.2 = (f32[5,64,128]{2,1,0:T(8,128)}, f32[5,64,128]{2,1,0:T(8,128)S(1)}, u32[]{:S(2)}, u32[]{:S(2)}) collective-permute-start(f32[5,64,128]{2,1,0:T(8,128)} %get-tuple-element.48), channel_id=1, source_target_pairs={{0,16},{8,24},{16,0},{24,8},{1,17},{9,25},{17,1},{25,9},{2,18},{10... | collective-permute-start | bytes 491528 | tf_op jit(solution)/shard_map/ppermute | solution.py:484
  21.3 0.5 collective-permute-start.3
  21.8 2.7 %spread.1 = f32[64,64,128]{2,1,0:T(8,128)} custom-call(s32[64]{0:T(128)} %send.1, f32[32,64,128]{2,1,0:T(8,128)} %get-tuple-element.40.coef), custom_call_target="tpu_custom_call" | custom-call | bytes 4000000 | tf_op jit(solution)/shard_map/spread/pallas_call | solution.py:158
  24.5 3.1 %collective-permute-done.5.refs_2_ = f32[584,128]{1,0:T(8,128)S(1)} collective-permute-done((f32[584,128]{1,0:T(8,128)}, f32[584,128]{1,0:T(8,128)S(1)}, u32[]{:S(2)}, u32[]{:S(2)}) %collective-permute-start.5) | collective-permute-done | bytes 299040 | tf_op jit(solution)/shard_map/ppermute | solution.py:460
  27.6 11.7 %collective-permute-done.4.refs_1_ = f32[584,128]{1,0:T(8,128)S(1)} collective-permute-done((f32[584,128]{1,0:T(8,128)}, f32[584,128]{1,0:T(8,128)S(1)}, u32[]{:S(2)}, u32[]{:S(2)}) %collective-permute-start.4) | collective-permute-done | bytes 299040 | tf_op jit(solution)/shard_map/ppermute | solution.py:460
  39.3 0.0 collective-permute-done.1.refs_1_
  39.4 0.0 collective-permute-done.2.refs_2_
  39.4 0.0 collective-permute-done.3.refs_3_
  39.4 4.9 %all-to-all-start = ((f32[64,64,128]{2,1,0:T(8,128)}), f32[64,64,128]{2,1,0:T(8,128)S(1)}, u32[]{:S(2)}, u32[]{:S(2)}) async-start(f32[64,64,128]{2,1,0:T(8,128)} %spread.1), calls=%async_computation | async-start | bytes 4194304 | tf_op jit(solution)/shard_map/all_to_all | solution.py:491
  44.3 2.7 %select.31 = (f32[15,64,128]{2,1,0:T(8,128)}, f32[15,64,128]{2,1,0:T(8,128)}, f32[15,64,128]{2,1,0:T(8,128)}, f32[15,64,128]{2,1,0:T(8,128)}) custom-call(s32[1]{0:T(128)} %bitcast.group_at, s32[1]{0:T(128)} %bitcast.1.lane_at.position, f32[584,128]{1,0:T(8,128)} %copy-done.5, f32[584,128]{1,0:T(8,128)} %copy-done.7, f32[584,128]{1,0:T(8,128)} %copy-done.6), custom_call_target="tpu_custom_call" | custom-call | bytes 4000000 | tf_op jit(solution)/shard_map/select/pallas_call | solution.py:208
  47.0 1.8 %collective-permute-start.6 = (f32[15,64,128]{2,1,0:T(8,128)}, f32[15,64,128]{2,1,0:T(8,128)S(1)}, u32[]{:S(2)}, u32[]{:S(2)}) collective-permute-start(f32[15,64,128]{2,1,0:T(8,128)} %get-tuple-element.54), channel_id=1, source_target_pairs={{0,8},{8,0},{16,24},{24,16},{1,9},{9,1},{17,25},{25,17},{2,10},{10... | collective-permute-start | bytes 1474568 | tf_op jit(solution)/shard_map/ppermute | solution.py:484
  48.9 1.5 %collective-permute-start.11 = (f32[15,64,128]{2,1,0:T(8,128)}, f32[15,64,128]{2,1,0:T(8,128)}, u32[]{:S(2)}, u32[]{:S(2)}) collective-permute-start(f32[15,64,128]{2,1,0:T(8,128)} %get-tuple-element.65), channel_id=1, source_target_pairs={{0,16},{8,24},{16,0},{24,8},{1,17},{9,25},{17,1},{25,9},{2,18},{10... | collective-permute-start | bytes 1474568 | tf_op jit(solution)/shard_map/ppermute | solution.py:484
  50.3 0.3 collective-permute-start.12
  50.6 0.2 dynamic-slice_reduce_fusion
  50.8 0.0 copy-start.17
  50.8 0.0 copy-start.16
  50.8 0.0 copy-start.1
  50.8 0.0 copy-start.2
  50.8 12.3 %prepare.1 = (bf16[32,128,832]{2,1,0:T(8,128)(2,1)}, bf16[32,256,128]{2,1,0:T(8,128)(2,1)}, bf16[8,128,2112]{2,1,0:T(8,128)(2,1)}) custom-call(f32[584,128]{1,0:T(8,128)} %get-tuple-element.45.after, f32[32,64,768]{2,1,0:T(8,128)} %coupling.1, f32[32,64,256]{2,1,0:T(8,128)} %basis.3, f32[32,64,64]{2,1,0:T(8,128)} %transfer.3, f32[8,64,2048]{2,1,0:T(8,128)} %mid_coupling.1, ...), custom_call_target="tpu_custom_call" | custom-call | bytes 30000000 | tf_op jit(solution)/shard_map/prepare/pallas_call | solution.py:245
  63.1 0.0 collective-permute-start.7
  63.2 0.5 collective-permute-start.8
  63.7 0.8 collective-permute-done.7.refs_8_
  64.6 0.1 collective-permute-start.9
  64.7 0.1 collective-permute-done.8.refs_9_
  64.8 0.3 collective-permute-start.10
  65.1 0.9 collective-permute-done.9.refs_10_
  66.0 0.1 collective-permute-start.13
  66.1 0.3 collective-permute-done.10.refs_11_
  66.4 8.4 %collective-permute-done.6.refs_5_ = f32[15,64,128]{2,1,0:T(8,128)S(1)} collective-permute-done((f32[15,64,128]{2,1,0:T(8,128)}, f32[15,64,128]{2,1,0:T(8,128)S(1)}, u32[]{:S(2)}, u32[]{:S(2)}) %collective-permute-start.6) | collective-permute-done | bytes 491552 | tf_op jit(solution)/shard_map/ppermute | solution.py:484
  74.8 3.1 %collective-permute-done.11.refs_6_ = f32[15,64,128]{2,1,0:T(8,128)} collective-permute-done((f32[15,64,128]{2,1,0:T(8,128)}, f32[15,64,128]{2,1,0:T(8,128)}, u32[]{:S(2)}, u32[]{:S(2)}) %collective-permute-start.11) | collective-permute-done | bytes 491552 | tf_op jit(solution)/shard_map/ppermute | solution.py:484
  77.9 0.0 collective-permute-start.15
  77.9 12.2 %collective-permute-done.12.refs_7_ = f32[15,64,128]{2,1,0:T(8,128)} collective-permute-done((f32[15,64,128]{2,1,0:T(8,128)}, f32[15,64,128]{2,1,0:T(8,128)}, u32[]{:S(2)}, u32[]{:S(2)}) %collective-permute-start.12) | collective-permute-done | bytes 491552 | tf_op jit(solution)/shard_map/ppermute | solution.py:484
  90.0 0.0 collective-permute-start.16
  90.1 0.5 collective-permute-start.14
  90.6 0.1 copy.15.pair_leaf
  90.7 0.0 collective-permute-done.13.refs_12_
  90.7 0.0 collective-permute-done.15.refs_14_
  90.7 1.6 %collective-permute-done.16.refs_15_ = f32[15,64,128]{2,1,0:T(8,128)} collective-permute-done((f32[15,64,128]{2,1,0:T(8,128)}, f32[15,64,128]{2,1,0:T(8,128)}, u32[]{:S(2)}, u32[]{:S(2)}) %collective-permute-start.16) | collective-permute-done | bytes 491552 | tf_op jit(solution)/shard_map/ppermute | solution.py:497
  92.3 0.5 collective-permute-done.14.refs_13_
  92.7 1.6 %all-to-all-done.refs_16_ = f32[64,64,128]{2,1,0:T(8,128)S(1)} async-done(((f32[64,64,128]{2,1,0:T(8,128)}), f32[64,64,128]{2,1,0:T(8,128)S(1)}, u32[]{:S(2)}, u32[]{:S(2)}) %all-to-all-start) | async-done | bytes 2097184 | tf_op jit(solution)/shard_map/all_to_all | solution.py:491
  94.4 12.7 %tail.1 = f32[8192,128]{1,0:T(8,128)} custom-call(s32[32]{0:T(128)S(1)} %copy-done.1, s32[8,32]{1,0:T(8,128)S(1)} %fusion.7.pair, s32[1]{0:T(128)} %bitcast.1.lane_at.position, s32[4]{0:T(128)S(1)} %and_select_fusion.3.tops, s32[32]{0:T(128)S(1)} %copy-done.2, s32[32,12]{1,0:T(8,128)S(1)} %copy.15.pair_leaf, f32[5,64,128]{2,1,0:T(8,128)} %get-tuple-element.55.refs_0_, ...), custom_call_target="tpu_custom_call" | custom-call | flops 6000000000 | bytes 20000000 | tf_op jit(solution)/shard_map/tail/pallas_call | solution.py:422
  (33 shorter events, 0.1 us)
Async XLA Ops:
  0.0 50.6 %copy-start = (s32[8,4]{0,1:T(4,128)S(1)}, s32[8,4]{0,1:T(4,128)}, u32[]{:S(2)}) copy-start(s32[8,4]{0,1:T(4,128)} %param.26) | copy-start | bytes 388
  7.4 10.9 %collective-permute-start = (f32[584,128]{1,0:T(8,128)}, f32[584,128]{1,0:T(8,128)S(1)}, u32[]{:S(2)}, u32[]{:S(2)}) collective-permute-start(f32[584,128]{1,0:T(8,128)} %get-tuple-element.45.after), channel_id=1, source_target_pairs={{0,2},{1,3},{2,0},{3,1},{4,6},{5,7},{6,4},{7,5},{8,10},{9,11},{10,... | collective-permute-start | bytes 897032 | tf_op jit(solution)/shard_map/ppermute | solution.py:460
  10.5 17.2 %collective-permute-start.5 = (f32[584,128]{1,0:T(8,128)}, f32[584,128]{1,0:T(8,128)S(1)}, u32[]{:S(2)}, u32[]{:S(2)}) collective-permute-start(f32[584,128]{1,0:T(8,128)} %get-tuple-element.45.after), channel_id=1, source_target_pairs={{0,6},{1,7},{2,4},{3,5},{4,2},{5,3},{6,0},{7,1},{8,14},{9,15},{10,... | collective-permute-start | bytes 897032 | tf_op jit(solution)/shard_map/ppermute | solution.py:460
  12.9 26.4 %collective-permute-start.4 = (f32[584,128]{1,0:T(8,128)}, f32[584,128]{1,0:T(8,128)S(1)}, u32[]{:S(2)}, u32[]{:S(2)}) collective-permute-start(f32[584,128]{1,0:T(8,128)} %get-tuple-element.45.after), channel_id=1, source_target_pairs={{0,4},{1,5},{2,6},{3,7},{4,0},{5,1},{6,2},{7,3},{8,12},{9,13},{10,... | collective-permute-start | bytes 897032 | tf_op jit(solution)/shard_map/ppermute | solution.py:460
  18.3 26.0 %copy-start.5 = (f32[584,128]{1,0:T(8,128)}, f32[584,128]{1,0:T(8,128)S(1)}, u32[]{:S(2)}) copy-start(f32[584,128]{1,0:T(8,128)S(1)} %collective-permute-done.refs_0_) | copy-start | bytes 897028
  18.3 21.1 %collective-permute-start.1 = (f32[5,64,128]{2,1,0:T(8,128)}, f32[5,64,128]{2,1,0:T(8,128)S(1)}, u32[]{:S(2)}, u32[]{:S(2)}) collective-permute-start(f32[5,64,128]{2,1,0:T(8,128)} %get-tuple-element.47), channel_id=1, source_target_pairs={{0,8},{8,0},{16,24},{24,16},{1,9},{9,1},{17,25},{25,17},{2,10},{10... | collective-permute-start | bytes 491528 | tf_op jit(solution)/shard_map/ppermute | solution.py:484
  19.8 19.6 %collective-permute-start.2 = (f32[5,64,128]{2,1,0:T(8,128)}, f32[5,64,128]{2,1,0:T(8,128)S(1)}, u32[]{:S(2)}, u32[]{:S(2)}) collective-permute-start(f32[5,64,128]{2,1,0:T(8,128)} %get-tuple-element.48), channel_id=1, source_target_pairs={{0,16},{8,24},{16,0},{24,8},{1,17},{9,25},{17,1},{25,9},{2,18},{10... | collective-permute-start | bytes 491528 | tf_op jit(solution)/shard_map/ppermute | solution.py:484
  21.3 18.1 %collective-permute-start.3 = (f32[5,64,128]{2,1,0:T(8,128)}, f32[5,64,128]{2,1,0:T(8,128)}, u32[]{:S(2)}, u32[]{:S(2)}) collective-permute-start(f32[5,64,128]{2,1,0:T(8,128)} %get-tuple-element.49), channel_id=1, source_target_pairs={{0,24},{8,16},{16,8},{24,0},{1,25},{9,17},{17,9},{25,1},{2,26},{10... | collective-permute-start | bytes 491528 | tf_op jit(solution)/shard_map/ppermute | solution.py:484
  27.6 16.6 %copy-start.6 = (f32[584,128]{1,0:T(8,128)}, f32[584,128]{1,0:T(8,128)S(1)}, u32[]{:S(2)}) copy-start(f32[584,128]{1,0:T(8,128)S(1)} %collective-permute-done.5.refs_2_) | copy-start | bytes 897028
  39.3 4.9 %copy-start.7 = (f32[584,128]{1,0:T(8,128)}, f32[584,128]{1,0:T(8,128)S(1)}, u32[]{:S(2)}) copy-start(f32[584,128]{1,0:T(8,128)S(1)} %collective-permute-done.4.refs_1_) | copy-start | bytes 897028
  39.3 23.8 %copy-start.9 = (f32[5,64,128]{2,1,0:T(8,128)}, f32[5,64,128]{2,1,0:T(8,128)S(1)}, u32[]{:S(2)}) copy-start(f32[5,64,128]{2,1,0:T(8,128)S(1)} %collective-permute-done.1.refs_1_) | copy-start | bytes 491524
  39.4 7.7 %copy-start.10 = (f32[5,64,128]{2,1,0:T(8,128)}, f32[5,64,128]{2,1,0:T(8,128)S(1)}, u32[]{:S(2)}) copy-start(f32[5,64,128]{2,1,0:T(8,128)S(1)} %collective-permute-done.2.refs_2_) | copy-start | bytes 491524
  39.4 55.0 %all-to-all-start = ((f32[64,64,128]{2,1,0:T(8,128)}), f32[64,64,128]{2,1,0:T(8,128)S(1)}, u32[]{:S(2)}, u32[]{:S(2)}) async-start(f32[64,64,128]{2,1,0:T(8,128)} %spread.1), calls=%async_computation | async-start | bytes 4194304 | tf_op jit(solution)/shard_map/all_to_all | solution.py:491
  47.0 27.8 %collective-permute-start.6 = (f32[15,64,128]{2,1,0:T(8,128)}, f32[15,64,128]{2,1,0:T(8,128)S(1)}, u32[]{:S(2)}, u32[]{:S(2)}) collective-permute-start(f32[15,64,128]{2,1,0:T(8,128)} %get-tuple-element.54), channel_id=1, source_target_pairs={{0,8},{8,0},{16,24},{24,16},{1,9},{9,1},{17,25},{25,17},{2,10},{10... | collective-permute-start | bytes 1474568 | tf_op jit(solution)/shard_map/ppermute | solution.py:484
  48.9 29.0 %collective-permute-start.11 = (f32[15,64,128]{2,1,0:T(8,128)}, f32[15,64,128]{2,1,0:T(8,128)}, u32[]{:S(2)}, u32[]{:S(2)}) collective-permute-start(f32[15,64,128]{2,1,0:T(8,128)} %get-tuple-element.65), channel_id=1, source_target_pairs={{0,16},{8,24},{16,0},{24,8},{1,17},{9,25},{17,1},{25,9},{2,18},{10... | collective-permute-start | bytes 1474568 | tf_op jit(solution)/shard_map/ppermute | solution.py:484
  50.3 39.7 %collective-permute-start.12 = (f32[15,64,128]{2,1,0:T(8,128)}, f32[15,64,128]{2,1,0:T(8,128)}, u32[]{:S(2)}, u32[]{:S(2)}) collective-permute-start(f32[15,64,128]{2,1,0:T(8,128)} %get-tuple-element.66), channel_id=1, source_target_pairs={{0,24},{8,16},{16,8},{24,0},{1,25},{9,17},{17,9},{25,1},{2,26},{10... | collective-permute-start | bytes 1474568 | tf_op jit(solution)/shard_map/ppermute | solution.py:484
  50.8 12.4 %copy-start.8 = (f32[5,64,128]{2,1,0:T(8,128)S(1)}, f32[5,64,128]{2,1,0:T(8,128)}, u32[]{:S(2)}) copy-start(f32[5,64,128]{2,1,0:T(8,128)} %get-tuple-element.55.refs_0_) | copy-start | bytes 491524
  50.8 12.9 %copy-start.17 = (s32[8,32]{1,0:T(8,128)S(1)}, s32[8,32]{1,0:T(8,128)}, u32[]{:S(2)}) copy-start(s32[8,32]{1,0:T(8,128)} %param.24) | copy-start | bytes 3076
  50.8 13.8 %copy-start.11 = (f32[5,64,128]{2,1,0:T(8,128)S(1)}, f32[5,64,128]{2,1,0:T(8,128)}, u32[]{:S(2)}) copy-start(f32[5,64,128]{2,1,0:T(8,128)} %copy-done.10) | copy-start | bytes 491524
  50.8 15.2 %copy-start.3 = (f32[15,64,128]{2,1,0:T(8,128)S(1)}, f32[15,64,128]{2,1,0:T(8,128)}, u32[]{:S(2)}) copy-start(f32[15,64,128]{2,1,0:T(8,128)} %get-tuple-element.63.refs_4_) | copy-start | bytes 1474564
  50.8 39.8 %copy-start.16 = (s32[32,12]{0,1:T(8,128)S(1)}, s32[32,12]{0,1:T(8,128)}, u32[]{:S(2)}) copy-start(s32[32,12]{0,1:T(8,128)} %param.21) | copy-start | bytes 4612
  50.8 43.6 %copy-start.1 = (s32[32]{0:T(128)S(1)}, s32[32]{0:T(128)}, u32[]{:S(2)}) copy-start(s32[32]{0:T(128)} %parent.3) | copy-start | bytes 388
  50.8 43.6 %copy-start.2 = (s32[32]{0:T(128)S(1)}, s32[32]{0:T(128)}, u32[]{:S(2)}) copy-start(s32[32]{0:T(128)} %size.3) | copy-start | bytes 388
  63.1 1.4 %collective-permute-start.7 = (f32[5,64,128]{2,1,0:T(8,128)S(1)}, f32[5,64,128]{2,1,0:T(8,128)S(1)}, u32[]{:S(2)}, u32[]{:S(2)}) collective-permute-start(f32[5,64,128]{2,1,0:T(8,128)S(1)} %copy-done.8), channel_id=1, source_target_pairs={{0,1},{1,0},{2,3},{3,2},{4,5},{5,4},{6,7},{7,6},{8,9},{9,8},{10,11... | collective-permute-start | bytes 491528 | tf_op jit(solution)/shard_map/ppermute | solution.py:492
  63.2 1.6 %collective-permute-start.8 = (f32[5,64,128]{2,1,0:T(8,128)S(1)}, f32[5,64,128]{2,1,0:T(8,128)S(1)}, u32[]{:S(2)}, u32[]{:S(2)}) collective-permute-start(f32[5,64,128]{2,1,0:T(8,128)S(1)} %collective-permute-done.1.refs_1_), channel_id=1, source_target_pairs={{0,1},{1,0},{2,3},{3,2},{4,5},{5,4},{6,7},{7,6},{8,9},{9,8},{10,11... | collective-permute-start | bytes 491528 | tf_op jit(solution)/shard_map/ppermute | solution.py:492
  64.6 25.5 %copy-start.12 = (f32[5,64,128]{2,1,0:T(8,128)}, f32[5,64,128]{2,1,0:T(8,128)S(1)}, u32[]{:S(2)}) copy-start(f32[5,64,128]{2,1,0:T(8,128)S(1)} %collective-permute-done.7.refs_8_) | copy-start | bytes 491524
  64.6 1.4 %collective-permute-start.9 = (f32[5,64,128]{2,1,0:T(8,128)S(1)}, f32[5,64,128]{2,1,0:T(8,128)S(1)}, u32[]{:S(2)}, u32[]{:S(2)}) collective-permute-start(f32[5,64,128]{2,1,0:T(8,128)S(1)} %copy-done.11), channel_id=1, source_target_pairs={{0,1},{1,0},{2,3},{3,2},{4,5},{5,4},{6,7},{7,6},{8,9},{9,8},{10,11... | collective-permute-start | bytes 491528 | tf_op jit(solution)/shard_map/ppermute | solution.py:492
  64.8 25.3 %copy-start.13 = (f32[5,64,128]{2,1,0:T(8,128)}, f32[5,64,128]{2,1,0:T(8,128)S(1)}, u32[]{:S(2)}) copy-start(f32[5,64,128]{2,1,0:T(8,128)S(1)} %collective-permute-done.8.refs_9_) | copy-start | bytes 491524
  64.8 1.6 %collective-permute-start.10 = (f32[5,64,128]{2,1,0:T(8,128)}, f32[5,64,128]{2,1,0:T(8,128)S(1)}, u32[]{:S(2)}, u32[]{:S(2)}) collective-permute-start(f32[5,64,128]{2,1,0:T(8,128)} %collective-permute-done.3.refs_3_), channel_id=1, source_target_pairs={{0,1},{1,0},{2,3},{3,2},{4,5},{5,4},{6,7},{7,6},{8,9},{9,8},{10,11... | collective-permute-start | bytes 491528 | tf_op jit(solution)/shard_map/ppermute | solution.py:492
  66.0 28.4 %copy-start.14 = (f32[5,64,128]{2,1,0:T(8,128)}, f32[5,64,128]{2,1,0:T(8,128)S(1)}, u32[]{:S(2)}) copy-start(f32[5,64,128]{2,1,0:T(8,128)S(1)} %collective-permute-done.9.refs_10_) | copy-start | bytes 491524
  66.0 24.7 %collective-permute-start.13 = (f32[15,64,128]{2,1,0:T(8,128)S(1)}, f32[15,64,128]{2,1,0:T(8,128)}, u32[]{:S(2)}, u32[]{:S(2)}) collective-permute-start(f32[15,64,128]{2,1,0:T(8,128)S(1)} %copy-done.3), channel_id=1, source_target_pairs={{0,1},{1,0},{2,3},{3,2},{4,5},{5,4},{6,7},{7,6},{8,9},{9,8},{10,11... | collective-permute-start | bytes 1474568 | tf_op jit(solution)/shard_map/ppermute | solution.py:497
  66.4 28.0 %copy-start.15 = (f32[5,64,128]{2,1,0:T(8,128)}, f32[5,64,128]{2,1,0:T(8,128)S(1)}, u32[]{:S(2)}) copy-start(f32[5,64,128]{2,1,0:T(8,128)S(1)} %collective-permute-done.10.refs_11_) | copy-start | bytes 491524
  74.8 19.6 %copy-start.4 = (f32[15,64,128]{2,1,0:T(8,128)}, f32[15,64,128]{2,1,0:T(8,128)S(1)}, u32[]{:S(2)}) copy-start(f32[15,64,128]{2,1,0:T(8,128)S(1)} %collective-permute-done.6.refs_5_) | copy-start | bytes 1474564
  77.9 12.8 %collective-permute-start.15 = (f32[15,64,128]{2,1,0:T(8,128)}, f32[15,64,128]{2,1,0:T(8,128)}, u32[]{:S(2)}, u32[]{:S(2)}) collective-permute-start(f32[15,64,128]{2,1,0:T(8,128)} %collective-permute-done.11.refs_6_), channel_id=1, source_target_pairs={{0,1},{1,0},{2,3},{3,2},{4,5},{5,4},{6,7},{7,6},{8,9},{9,8},{10,11... | collective-permute-start | bytes 1474568 | tf_op jit(solution)/shard_map/ppermute | solution.py:497
  90.0 2.2 %collective-permute-start.16 = (f32[15,64,128]{2,1,0:T(8,128)}, f32[15,64,128]{2,1,0:T(8,128)}, u32[]{:S(2)}, u32[]{:S(2)}) collective-permute-start(f32[15,64,128]{2,1,0:T(8,128)} %collective-permute-done.12.refs_7_), channel_id=1, source_target_pairs={{0,1},{1,0},{2,3},{3,2},{4,5},{5,4},{6,7},{7,6},{8,9},{9,8},{10,11... | collective-permute-start | bytes 1474568 | tf_op jit(solution)/shard_map/ppermute | solution.py:497
  90.1 2.7 %collective-permute-start.14 = (f32[15,64,128]{2,1,0:T(8,128)S(1)}, f32[15,64,128]{2,1,0:T(8,128)}, u32[]{:S(2)}, u32[]{:S(2)}) collective-permute-start(f32[15,64,128]{2,1,0:T(8,128)S(1)} %collective-permute-done.6.refs_5_), channel_id=1, source_target_pairs={{0,1},{1,0},{2,3},{3,2},{4,5},{5,4},{6,7},{7,6},{8,9},{9,8},{10,11... | collective-permute-start | bytes 1474568 | tf_op jit(solution)/shard_map/ppermute | solution.py:497
